TPU v7x, 32 devices: a whole 2x2x4 slice. The times are simulated.
32 devices in a mesh: req: 8 (over z, y), tensor: 4 (over x, core).
Axes of the slice: x: 2, y: 2, z: 4, core: 2. Of those that a mesh axis runs over, the one named last changes fastest.
Arguments:
- hidden: bfloat16 [192, 16384], P('tensor', 'req'), may hold values from -6 to 6
- w_query: bfloat16 [16384, 8192], P('req', 'tensor'), may hold values from -0.046875 to 0.046875
- keyvalue_weight: bfloat16 [16384, 1024], P('req', 'tensor'), may hold values from -0.125 to 0.125
- w_out: bfloat16 [8192, 16384], P('tensor', 'req'), may hold values from -0.25 to 0.25
- keyvalue_cache: bfloat16 [8, 4096, 1024], P('req', 'tensor'), may hold values from -260 to 260
- cache_live: int32 [8, 256], P('req'), may hold values 0 or 1
- tree_size: int32 [8], replicated, may hold values from 1 to 48, 192 in all
- tree_parent: int32 [8, 48], replicated, may hold values from 0 to 46, as said below
- slot_request: int32 [8], replicated, may hold values from 0 to 7, each once
Outputs:
- mixed: bfloat16 [192, 16384], P('tensor', 'req')
Inputs may be any that keep to these rules, and one draw needn't show every extreme that they name: `tree_size`: the sizes add up to 192, and the largest is exactly 48. `tree_parent`: for node k >= 1 of a request's tree the parent is one of the nodes max(0, k - 4) .. k - 1; the entry of node 0, the root, is 0. Entries of nodes at or beyond the request's tree_size are present but belong to no node. `slot_request`: A permutation of the requests.
All inputs are finite; a program needn't handle non-finite values. No bound on the sum of `cache_live` on one device may be relied on, other than what follows from the above.
Results may differ from a plain program's by a relative error of at most 0.04.
Values may be sent and summed in bfloat16 or wider, within the bound.
A program may use at most 128 MiB of HBM per device.

v0:
```python
import math

import jax
import jax.numpy as jnp
from jax import lax
from jax.sharding import PartitionSpec as P

HEAD_SIZE = 128
QUERY_HEADS = 64
KEYVALUE_HEADS = 4
MOST_TREE_NODES = 48
CACHE_POSITIONS = 4096
CBLK = 16


ROPE_BASE = 500000.0
NEGATIVE = -1e30


def lookup(table_vals, index_vals):
    table_ids = jnp.arange(table_vals.shape[0], dtype=jnp.int32)
    return jnp.sum(
        jnp.where(index_vals[:, None] == table_ids[None, :], table_vals[None, :], 0), axis=1
    )


def ancestors(parents):
    node_ids = jnp.arange(MOST_TREE_NODES, dtype=jnp.int32)
    linked = (parents[..., :, None] == node_ids).astype(jnp.float32)
    identity = (node_ids[:, None] == node_ids[None, :]).astype(jnp.float32)
    closure = jnp.maximum(linked, identity)
    for sweep in range((MOST_TREE_NODES - 1).bit_length()):
        closure = jnp.minimum(jnp.matmul(closure, closure, precision=lax.Precision.HIGHEST), 1.0)
    return closure


def rotary(tree_depth):
    half_ids = jnp.arange(HEAD_SIZE // 2, dtype=jnp.float32)
    inv_freq = 1.0 / ROPE_BASE ** (half_ids * 2.0 / HEAD_SIZE)
    angles = (tree_depth + CACHE_POSITIONS)[..., None] * inv_freq
    angles = jnp.concatenate([angles, angles], axis=-1)
    return (jnp.cos(angles), jnp.sin(angles))


def rotate(values, cosine_table, sine_table):
    widened = values.astype(jnp.float32)
    lower_half, upper_half = jnp.split(widened, 2, axis=-1)
    turned = jnp.concatenate([-upper_half, lower_half], axis=-1)
    return widened * cosine_table[..., None, :] + turned * sine_table[..., None, :]


def body(
    hidden,
    w_query,
    keyvalue_weight,
    w_out,
    keyvalue_cache,
    cache_live,
    tree_size,
    tree_parent,
    slot_request,
):
    tensor_count = lax.axis_size("tensor")
    req_index = lax.axis_index("req")
    tensor_index = lax.axis_index("tensor")
    resident_requests = keyvalue_cache.shape[0]
    resident_slots = resident_requests * MOST_TREE_NODES
    row_total = hidden.shape[0] * tensor_count
    query_columns = w_query.shape[1]
    heads_here = query_columns // HEAD_SIZE
    query_group_size = QUERY_HEADS // KEYVALUE_HEADS
    score_scale = 1.0 / math.sqrt(HEAD_SIZE)
    kv_head = tensor_index * heads_here // query_group_size
    row_ends = jnp.cumsum(tree_size)
    starts = row_ends - tree_size
    request_ids = jnp.arange(tree_size.shape[0], dtype=jnp.int32)
    home_slot = jnp.sum(
        jnp.where(slot_request[None, :] == request_ids[:, None], request_ids[None, :], 0), axis=1
    )
    features = lax.all_gather(hidden, "tensor", axis=0, tiled=True)
    w_both = jnp.concatenate([w_query, keyvalue_weight], axis=1)
    slot_ids = jnp.arange(resident_slots * lax.axis_size("req"), dtype=jnp.int32)
    owner_req = lookup(slot_request, slot_ids // MOST_TREE_NODES)
    node_ids = slot_ids % MOST_TREE_NODES
    is_valid = node_ids < lookup(tree_size, owner_req)
    row_ids = jnp.minimum(lookup(starts, owner_req) + node_ids, row_total - 1)
    row_ids, is_valid = (row_ids, is_valid)
    occupied_rows = jnp.take(features, row_ids, axis=0)
    occupied_rows = jnp.where(is_valid[:, None], occupied_rows, jnp.zeros_like(occupied_rows))
    projected = lax.psum_scatter(
        jnp.dot(occupied_rows, w_both, preferred_element_type=jnp.float32).astype(jnp.bfloat16),
        "req",
        scatter_dimension=0,
        tiled=True,
    )
    query_here = projected[:, :query_columns]
    keyval_here = projected[:, query_columns:]
    my_requests = lax.dynamic_slice_in_dim(
        slot_request, req_index * resident_requests, resident_requests
    )
    parents = jnp.sum(
        jnp.where(
            my_requests[:, None, None] == request_ids[None, :, None], tree_parent[None, :, :], 0
        ),
        axis=1,
    )
    closure = ancestors(parents)
    tree_depth = jnp.sum(closure, axis=-1) - 1.0
    cosine_table, sine_table = rotary(tree_depth.reshape(resident_slots))
    tree_ok = (closure > 0.5)[:, :, None, :]
    keyvalue_every_head = lax.all_gather(keyval_here, "tensor", axis=1, tiled=True)
    query_mine = rotate(
        query_here.reshape(resident_slots, heads_here, HEAD_SIZE), cosine_table, sine_table
    ).astype(jnp.bfloat16)
    query_grid = query_mine.reshape(resident_requests, MOST_TREE_NODES, heads_here, HEAD_SIZE)
    cache_portion = lax.all_gather(keyvalue_cache, "tensor", axis=1, tiled=True)
    portion_length = cache_portion.shape[1]
    portion_rows = cache_portion.reshape(
        resident_requests, portion_length, KEYVALUE_HEADS, 2, HEAD_SIZE
    )
    head_rows = lax.dynamic_index_in_dim(portion_rows, kv_head, axis=2, keepdims=False)
    top_now = jnp.full((resident_requests, MOST_TREE_NODES, heads_here), NEGATIVE, jnp.float32)
    scores = (
        jnp.einsum(
            "rkhd,rpd->rkhp", query_grid, head_rows[:, :, 0], preferred_element_type=jnp.float32
        )
        * score_scale
    )
    live_mask = (jnp.repeat(cache_live, CBLK, axis=1) > 0)[:, None, None, :]
    top_next = jnp.maximum(top_now, jnp.max(jnp.where(live_mask, scores, NEGATIVE), axis=-1))
    weights = jnp.where(live_mask, jnp.exp(scores - top_next[..., None]), 0.0)
    sum_next = jnp.sum(weights, axis=-1)
    mix_next = jnp.einsum(
        "rkhp,rpd->rkhd",
        weights.astype(jnp.bfloat16),
        head_rows[:, :, 1],
        preferred_element_type=jnp.float32,
    )
    keyvalue_layout = keyvalue_every_head.reshape(resident_slots, 2, HEAD_SIZE, KEYVALUE_HEADS)
    head_kv = lax.dynamic_index_in_dim(keyvalue_layout, kv_head, axis=3, keepdims=False)
    key_mine = (
        rotate(head_kv[:, 0][:, None, :], cosine_table, sine_table)
        .astype(jnp.bfloat16)
        .reshape(resident_requests, MOST_TREE_NODES, HEAD_SIZE)
    )
    value_mine = head_kv[:, 1].reshape(resident_requests, MOST_TREE_NODES, HEAD_SIZE)
    query_block = query_mine.reshape(resident_requests, MOST_TREE_NODES, heads_here, HEAD_SIZE)
    tree_scores = (
        jnp.einsum("rkhd,rid->rkhi", query_block, key_mine, preferred_element_type=jnp.float32)
        * score_scale
    )
    top_score = jnp.maximum(top_next, jnp.max(jnp.where(tree_ok, tree_scores, NEGATIVE), axis=-1))
    rescale_cache = jnp.exp(top_next - top_score)
    tree_weights = jnp.where(tree_ok, jnp.exp(tree_scores - top_score[..., None]), 0.0)
    weight_total = sum_next * rescale_cache + jnp.sum(tree_weights, axis=-1)
    mix_total = mix_next * rescale_cache[..., None]
    mix_total = mix_total + jnp.einsum(
        "rkhi,rid->rkhd",
        tree_weights.astype(jnp.bfloat16),
        value_mine,
        preferred_element_type=jnp.float32,
    )
    attention = (
        (mix_total / weight_total[..., None])
        .astype(jnp.bfloat16)
        .reshape(resident_slots, heads_here * HEAD_SIZE)
    )
    slot_attention = lax.all_gather(attention, "req", axis=0, tiled=True)
    row_ids = jnp.arange(row_total // tensor_count * lax.axis_size("tensor"), dtype=jnp.int32)
    owner_req = jnp.sum((row_ends[None, :] <= row_ids[:, None]).astype(jnp.int32), axis=1)
    slot_ids = lookup(home_slot, owner_req) * MOST_TREE_NODES + row_ids - lookup(starts, owner_req)
    occupied_rows = jnp.take(slot_attention, slot_ids, axis=0)
    return lax.psum_scatter(
        jnp.dot(occupied_rows, w_out, preferred_element_type=jnp.float32).astype(jnp.bfloat16),
        "tensor",
        scatter_dimension=0,
        tiled=True,
    )


def solution(mesh):
    placed = (
        P("tensor", "req"),
        P("req", "tensor"),
        P("req", "tensor"),
        P("tensor", "req"),
        P("req", "tensor", None),
        P("req", None),
        P(),
        P(),
        P(),
    )
    return jax.shard_map(
        body, mesh=mesh, in_specs=placed, out_specs=P("tensor", "req"), check_vma=False
    )
```

profile of v0, /device:TPU:0, one launch (start us, length us, event | category | flops | bytes accessed | tf_op | source)
XLA Modules:
  0.0 218.2 jit_solution(16858175963958013880)
XLA Ops:
  7.4 0.0 reduce-scatter.3.cloned.1.call-start
  7.4 0.9 reduce-window.8
  8.3 0.7 bitcast_subtract_fusion
  9.0 0.7 select_reduce_fusion.4
  9.7 0.7 select_reduce_fusion.3
  10.5 10.3 %all_gather.12 = bf16[192,2048]{1,0:T(8,128)(2,1)S(1)} all-gather(bf16[48,2048]{1,0:T(8,128)(2,1)} %param.9), channel_id=1, replica_groups=mesh['req'=8,'tensor'=4] {'tensor'}, dimensions={0}, use_global_device_ids=true | all-gather | bytes 983040 | tf_op jit(solution)/shard_map/all_gather | solution.py:80
  20.8 2.4 %gather_fusion = bf16[384,2048]{1,0:T(8,128)(2,1)S(1)} fusion(bf16[192,2048]{1,0:T(8,128)(2,1)S(1)} %all_gather.12, s32[1024]{0:T(1024)S(1)} %pad_clamp_fusion.1), kind=kCustom, calls=%fused_computation | custom fusion | bytes 3147264 | tf_op jit(solution)/shard_map/jit(_take)/gather | solution.py:88
  23.2 0.0 copy-done.2
  23.2 0.0 copy-start.1
  23.2 0.0 copy-start.3
  23.2 0.0 copy-start
  23.3 8.6 %fusion.9 = bf16[384,2304]{1,0:T(8,128)(2,1)} fusion(bf16[2048,256]{1,0:T(8,128)(2,1)S(1)} %copy-done.2, bf16[2048,2048]{1,0:T(8,128)(2,1)} %param.10, bf16[384,2048]{1,0:T(8,128)(2,1)S(1)} %gather_fusion, pred[384]{0:T(512)(128)(4,1)S(1)} %get-tuple-element.28, pred[384]{0:T(512)(128)(4,1)S(1)} %get-tuple-element.27), kind=kOutput, calls=%fused_computation.12 | convolution fusion | flops 3645210624 | bytes 12780288 | tf_op jit(solution)/shard_map/dot_general | solution.py:91
  31.9 0.0 reduce-scatter.3.cloned.1.call-update
  31.9 0.0 all-gather.3.cloned.1.call-start
  32.0 0.5 all-gather.3.cloned.1.call-update
  32.5 0.0 all-gather.5.cloned.1.call-start
  32.6 0.0 copy-done.1
  32.6 0.6 dynamic_slice.11
  33.2 0.1 broadcast_in_dim.192
  33.3 0.1 gt.29
  33.4 0.7 iota_compare_fusion.5
  34.1 0.1 select_reduce_fusion.7
  34.2 0.1 fusion.36
  34.3 0.1 convolution_minimum_fusion.5
  34.5 0.2 convolution_minimum_fusion.4
  34.6 0.2 convolution_minimum_fusion.3
  34.8 0.2 convolution_minimum_fusion.2
  35.0 0.2 convolution_minimum_fusion.1
  35.1 0.3 fusion.61
  35.4 0.1 fusion.43
  35.5 0.2 fusion.40
  35.7 63.3 %reduce-scatter.3.cloned.1.call-done = bf16[48,2304]{1,0:T(8,128)(2,1)} async-done(((bf16[384,2304]{1,0:T(8,128)(2,1)}), bf16[48,2304]{1,0:T(8,128)(2,1)}) %reduce-scatter.3.cloned.1.call-update) | async-done | bytes 221200 | tf_op jit(solution)/shard_map/reduce_scatter | solution.py:90
  99.0 0.7 slice.31
  99.7 5.5 %all_gather.14 = bf16[48,1024]{1,0:T(8,128)(2,1)S(1)} all-gather(bf16[48,256]{1,0:T(8,128)(2,1)S(1)} %slice.31), channel_id=1, replica_groups=mesh['req'=8,'tensor'=4] {'tensor'}, dimensions={1}, use_global_device_ids=true | all-gather | bytes 122880 | tf_op jit(solution)/shard_map/all_gather | solution.py:111
  105.2 0.2 copy.19
  105.4 0.1 constant_dynamic-slice_fusion
  105.5 0.1 copy.20
  105.6 1.0 convert_bitcast_fusion
  106.6 0.1 copy.24
  106.7 0.2 slice_negate_fusion
  106.9 0.2 maximum_multiply_fusion
  107.1 1.2 fusion.32
  108.3 0.1 slice_negate_fusion.1
  108.4 0.5 select_reduce_fusion.1
  108.9 0.0 all-gather.3.cloned.1.call-done
  108.9 14.3 %reshape.604 = bf16[1,4096,4,2,128]{4,3,2,1,0:T(2,128)(2,1)} reshape(bf16[1,4096,1024]{2,1,0:T(8,128)(2,1)} %all-gather.3.cloned.1.call-done) | data formatting | bytes 16777216 | tf_op jit(solution)/shard_map/reshape | solution.py:118
  123.3 3.2 %constant_dynamic-slice_fusion.1 = bf16[1,4096,1,2,128]{4,3,2,1,0:T(2,128)(2,1)S(1)} fusion(bf16[1,4096,4,2,128]{4,3,2,1,0:T(2,128)(2,1)} %reshape.604, s32[]{:T(128)S(6)} %select_n.149), kind=kLoop, calls=%fused_computation.113 | loop fusion | bytes 4194308 | tf_op jit(solution)/shard_map/jit(dynamic_index_in_dim)/dynamic_slice | solution.py:121
  126.5 0.3 copy.36
  126.8 2.2 %select_reduce_fusion = (f32[48,16]{1,0:T(8,128)S(1)}, f32[48,16,4096]{2,1,0:T(8,128)S(1)}) fusion(pred[4096]{0:T(1024)(128)(4,1)S(1)} %gt.29, bf16[48,16,128]{2,1,0:T(8,128)(2,1)S(1)} %bitcast.76, bf16[1,4096,2,128]{3,1,2,0:T(8,128)(2,1)S(1)} %bitcast.72), kind=kOutput, calls=%fused_computation.3 | convolution fusion | flops 814742784 | bytes 13835264 | tf_op jit(solution)/shard_map/rkhd,rpd->rkhp/dot_general | solution.py:124
  129.0 0.3 fusion.29
  129.3 3.1 %fusion = f32[48,16]{1,0:T(8,128)S(1)} fusion(f32[48,16,4096]{2,1,0:T(8,128)S(1)} %get-tuple-element.26, f32[48,16]{1,0:T(8,128)S(1)} %get-tuple-element.14, pred[4096]{0:T(1024)(128)(4,1)S(1)} %gt.29), kind=kLoop, calls=%fused_computation.4 | loop fusion | flops 12582144 | bytes 12593152 | tf_op jit(solution)/shard_map/reduce_sum | solution.py:132
  132.5 2.1 fusion.17
  134.7 0.3 fusion.20
  135.0 0.7 copy.37
  135.7 0.0 all-gather.5.cloned.1.call-update
  135.7 0.0 reduce-scatter.5.cloned.1.call-start
  135.8 0.1 select_reduce_fusion.8
  135.9 0.1 convert_reduce_fusion
  136.0 0.1 select_reduce_fusion.6
  136.1 42.9 %all-gather.5.cloned.1.call-done = bf16[384,2048]{1,0:T(8,128)(2,1)} async-done(((bf16[48,2048]{1,0:T(8,128)(2,1)}), bf16[384,2048]{1,0:T(8,128)(2,1)}) %all-gather.5.cloned.1.call-update) | async-done | bytes 1572880 | tf_op jit(solution)/shard_map/all_gather | solution.py:168
  179.0 3.5 %gather_fusion.1 = bf16[192,2048]{1,0:T(8,128)(2,1)S(1)} fusion(bf16[384,2048]{1,0:T(8,128)(2,1)} %all-gather.5.cloned.1.call-done, s32[1024]{0:T(1024)S(1)} %pad_clamp_fusion), kind=kCustom, calls=%fused_computation.1 | custom fusion | bytes 1573632 | tf_op jit(solution)/shard_map/jit(_take)/gather | solution.py:172
  182.5 6.1 %convolution_convert_fusion = bf16[192,2048]{1,0:T(8,128)(2,1)} fusion(bf16[2048,2048]{1,0:T(8,128)(2,1)} %param.12, bf16[192,2048]{1,0:T(8,128)(2,1)S(1)} %gather_fusion.1, pred[192]{0:T(512)(128)(4,1)S(1)} %compare_and_fusion.1), kind=kOutput, calls=%fused_computation.13 | convolution fusion | flops 1611399168 | bytes 9961664 | tf_op jit(solution)/shard_map/dot_general | solution.py:174
  188.6 0.0 reduce-scatter.5.cloned.1.call-update
  188.7 22.1 %reduce-scatter.5.cloned.1.call-done = bf16[48,2048]{1,0:T(8,128)(2,1)} async-done(((bf16[192,2048]{1,0:T(8,128)(2,1)}), bf16[48,2048]{1,0:T(8,128)(2,1)}) %reduce-scatter.5.cloned.1.call-update) | async-done | bytes 196624 | tf_op jit(solution)/shard_map/reduce_scatter | solution.py:173
  (20 shorter events, 0.2 us)
Async XLA Ops:
  7.4 15.8 %copy-start.2 = (bf16[2048,256]{1,0:T(8,128)(2,1)S(1)}, bf16[2048,256]{1,0:T(8,128)(2,1)}, u32[]{:S(2)}) copy-start(bf16[2048,256]{1,0:T(8,128)(2,1)} %param.11) | copy-start | bytes 3145732
  7.4 91.6 %reduce-scatter.3.cloned.1.call-start = ((), (), s32[]{:S(2)}) async-start(), calls=%async_computation.2 | async-start | bytes 1990656 | tf_op jit(solution)/shard_map/reduce_scatter | solution.py:90
  23.2 9.3 %copy-start.1 = (s32[8]{0:T(128)S(1)}, s32[8]{0:T(128)}, u32[]{:S(2)}) copy-start(s32[8]{0:T(128)} %param.17) | copy-start | bytes 100
  23.2 9.9 %copy-start.3 = (s32[1,256]{1,0:T(1,128)S(1)}, s32[1,256]{1,0:T(1,128)}, u32[]{:S(2)}) copy-start(s32[1,256]{1,0:T(1,128)} %param.14) | copy-start | bytes 3076
  23.2 10.8 %copy-start = (s32[8,48]{1,0:T(8,128)S(1)}, s32[8,48]{1,0:T(8,128)}, u32[]{:S(2)}) copy-start(s32[8,48]{1,0:T(8,128)} %param.16) | copy-start | bytes 4612
  31.9 77.0 %all-gather.3.cloned.1.call-start = ((), (), s32[]{:S(2)}) async-start(), calls=%async_computation.3 | async-start | bytes 10485760 | tf_op jit(solution)/shard_map/all_gather | solution.py:116
  32.5 146.5 %all-gather.5.cloned.1.call-start = ((), (), s32[]{:S(2)}) async-start(), calls=%async_computation.4 | async-start | bytes 1769472 | tf_op jit(solution)/shard_map/all_gather | solution.py:168
  135.7 75.0 %reduce-scatter.5.cloned.1.call-start = ((), (), s32[]{:S(2)}) async-start(), calls=%async_computation.5 | async-start | bytes 983040 | tf_op jit(solution)/shard_map/reduce_scatter | solution.py:173
Sparse Core Ops, SparseCore 0:
  32.0 66.8 reduce-scatter.2
  135.8 43.0 all-gather.4
Sparse Core Ops, SparseCore 1:
  34.0 59.1 all-gather.2
  188.7 21.9 reduce-scatter.4
where the time goes:
time: 219 us; the launch traced here: 218 us
  waiting for transfers between devices  129 us (59%)
  local copies, waits for them, and re-layouts  26.6 us (12%)
  matrix products  20.9 us (10%)
  blocking collectives  15.8 us (7%)
  between operations  15.2 us (7%)
  other arithmetic  10.7 us (5%)
    reduce_scatter x1, waiting for transfers between devices, body(): lax.psum_scatter(jnp.dot(occupied_rows, w_both, preferred_element_type=jn...  63.3 us
    all_gather x1, waiting for transfers between devices, body(): slot_attention = lax.all_gather(attention, 'req', axis=0, tiled=True)  42.9 us
    reduce_scatter x1, waiting for transfers between devices, body(): lax.psum_scatter(jnp.dot(occupied_rows, w_out, preferred_element_type=jnp...  22.1 us
    reshape x1, local copies, waits for them, and re-layouts, body(): cache_portion.reshape(resident_requests, portion_length, KEYVALUE_HEADS,...  14.3 us
    all_gather x1, blocking collectives, body(): features = lax.all_gather(hidden, 'tensor', axis=0, tiled=True)  10.3 us
    dot_general x1, matrix products, body(): jnp.dot(occupied_rows, w_both, preferred_element_type=jnp.float32)  8.63 us
    dot_general x1, matrix products, body(): jnp.dot(occupied_rows, w_out, preferred_element_type=jnp.float32)  6.13 us
    all_gather x1, blocking collectives, body(): lax.all_gather(keyval_here, 'tensor', axis=1, tiled=True)  5.5 us
  transfers between devices with their start and end apart: 4, of which 3 were waited for; matrix products, arithmetic and copies ran while one was open for 3% of the time, Pallas kernels for 0%

commit v1 on v0

--- a/solution.py
+++ b/solution.py
@@ -1,8 +1,11 @@
+import functools
 import math
 
 import jax
 import jax.numpy as jnp
 from jax import lax
+from jax.experimental import pallas as pl
+from jax.experimental.pallas import tpu as pltpu
 from jax.sharding import PartitionSpec as P
 
 HEAD_SIZE = 128
@@ -47,6 +50,420 @@
     lower_half, upper_half = jnp.split(widened, 2, axis=-1)
     turned = jnp.concatenate([-upper_half, lower_half], axis=-1)
     return widened * cosine_table[..., None, :] + turned * sine_table[..., None, :]
+
+
+MESH = pl.DeviceIdType.MESH
+VMEM_BYTES = 56 * 1024 * 1024
+
+
+def inner_of(count):
+    inner = 1
+    while inner * inner * 4 <= count:
+        inner *= 2
+    return inner
+
+
+def target(axis, index):
+    other = "tensor" if axis == "req" else "req"
+    return {axis: index, other: lax.axis_index(other)}
+
+
+def place(axis, inner):
+    count = lax.axis_size(axis)
+    me = lax.axis_index(axis)
+    outer = count // inner
+    major, minor = me // inner, lax.rem(me, inner)
+
+    def at(step_major, step_minor):
+        return lax.rem(major + step_major + outer, outer) * inner + lax.rem(
+            minor + step_minor + inner, inner
+        )
+
+    return outer, at
+
+
+def greet(axes):
+    barrier = pltpu.get_barrier_semaphore()
+    greeted = 0
+    for axis, inner in axes:
+        outer, at = place(axis, inner)
+        steps = [(d, 0) for d in range(1, outer)] + [(0, e) for e in range(1, inner)]
+        for d, e in steps:
+            pl.semaphore_signal(
+                barrier, inc=1, device_id=target(axis, at(d, e)), device_id_type=MESH
+            )
+            greeted += 1
+    pl.semaphore_wait(barrier, greeted)
+
+
+def remote(source, landing, sends, recvs, slot, axis, index):
+    return pltpu.make_async_remote_copy(
+        src_ref=source,
+        dst_ref=landing,
+        send_sem=sends.at[slot],
+        recv_sem=recvs.at[slot],
+        device_id=target(axis, index),
+        device_id_type=MESH,
+    )
+
+
+def start_gather(axis, inner, own, part, sends, recvs):
+    outer, at = place(axis, inner)
+    started = []
+    for d in range(1, outer):
+        copy = remote(own, part(at(0, 0)), sends, recvs, d, axis, at(d, 0))
+        copy.start()
+        started.append(copy)
+    for e in range(1, inner):
+        copy = remote(own, part(at(0, 0)), sends, recvs, e * outer, axis, at(0, e))
+        copy.start()
+        started.append(copy)
+    return started
+
+
+def finish_gather(axis, inner, own, part, sends, recvs, started):
+    outer, at = place(axis, inner)
+    for d in range(1, outer):
+        landed = part(at(-d, 0))
+        remote(own, landed, sends, recvs, d, axis, at(d, 0)).wait_recv()
+        for e in range(1, inner):
+            copy = remote(landed, landed, sends, recvs, e * outer + d, axis, at(0, e))
+            copy.start()
+            started.append(copy)
+    for e in range(1, inner):
+        for d in range(outer):
+            landed = part(at(-d, -e))
+            remote(own, landed, sends, recvs, e * outer + d, axis, at(0, e)).wait_recv()
+    for copy in started:
+        copy.wait_send()
+
+
+def sum_scatter(axis, inner, produce, part, near, staged, far, sends, recvs, finish):
+    outer, at = place(axis, inner)
+    order = list(range(1, outer)) + [0]
+    started = []
+    for d in order:
+        for e in range(1, inner):
+            index = at(d, e)
+            produce(index)
+            copy = remote(
+                part(index),
+                near.at[(e - 1) * outer + d],
+                sends,
+                recvs,
+                e * outer + d,
+                axis,
+                at(0, e),
+            )
+            copy.start()
+            started.append(copy)
+    for d in order:
+        produce(at(d, 0))
+    total = None
+    for d in order:
+        block = part(at(d, 0))
+        total = block[...].astype(jnp.float32)
+        for e in range(1, inner):
+            slot = (e - 1) * outer + d
+            remote(
+                block, near.at[slot], sends, recvs, e * outer + d, axis, at(0, e)
+            ).wait_recv()
+            total = total + near[slot].astype(jnp.float32)
+        if d:
+            staged[d - 1] = total.astype(jnp.bfloat16)
+            copy = remote(
+                staged.at[d - 1], far.at[d - 1], sends, recvs, d, axis, at(d, 0)
+            )
+            copy.start()
+            started.append(copy)
+    for d in range(1, outer):
+        remote(
+            staged.at[d - 1], far.at[d - 1], sends, recvs, d, axis, at(d, 0)
+        ).wait_recv()
+        total = total + far[d - 1].astype(jnp.float32)
+    finish(total.astype(jnp.bfloat16))
+    for copy in started:
+        copy.wait_send()
+
+
+def tiles(width):
+    step = 256 if width % 256 == 0 else width
+    return width // step, step
+
+
+def project_kernel(
+    req_inner,
+    core_inner,
+    group_size,
+    hidden_ref,
+    pick_ref,
+    wq_ref,
+    wkv_ref,
+    cache_ref,
+    query_ref,
+    kv_ref,
+    kvcache_ref,
+    rows,
+    wq,
+    wkv,
+    product,
+    blocks,
+    near,
+    staged,
+    far,
+    load_sem,
+    row_send,
+    row_recv,
+    cache_send,
+    cache_recv,
+    sum_send,
+    sum_recv,
+    kv_send,
+    kv_recv,
+):
+    tensor_count = lax.axis_size("tensor")
+    me = lax.axis_index("tensor")
+    rows_here = hidden_ref.shape[0]
+    query_columns = wq.shape[1]
+    heads_here = query_columns // HEAD_SIZE
+    pair = 2 * HEAD_SIZE
+    positions = cache_ref.shape[0]
+    load_q = pltpu.make_async_copy(wq_ref, wq, load_sem.at[0])
+    load_kv = pltpu.make_async_copy(wkv_ref, wkv, load_sem.at[1])
+    load_q.start()
+    load_kv.start()
+    greet([("tensor", tensor_count), ("req", req_inner)])
+
+    def row_part(index):
+        return rows.at[pl.ds(pl.multiple_of(index * rows_here, rows_here), rows_here)]
+
+    started = start_gather("tensor", core_inner, hidden_ref, row_part, row_send, row_recv)
+    rows[pl.ds(pl.multiple_of(me * rows_here, rows_here), rows_here), :] = hidden_ref[...]
+    finish_gather("tensor", core_inner, hidden_ref, row_part, row_send, row_recv, started)
+
+    def cache_part(owner, reader):
+        head = reader * heads_here // group_size
+        return (
+            cache_ref.at[:, pl.ds(pl.multiple_of(head * pair, pair), pair)],
+            kvcache_ref.at[pl.ds(pl.multiple_of(owner * positions, positions), positions)],
+        )
+
+    source, landing = cache_part(me, me)
+    own_cache = pltpu.make_async_copy(source, landing, load_sem.at[2])
+    own_cache.start()
+    cache_copies = []
+    for step in range(1, tensor_count):
+        reader = lax.rem(me + step, tensor_count)
+        source, landing = cache_part(me, reader)
+        copy = remote(source, landing, cache_send, cache_recv, step, "tensor", reader)
+        copy.start()
+        cache_copies.append(copy)
+
+    load_q.wait()
+    load_kv.wait()
+    steps, step_width = tiles(query_columns)
+
+    @pl.loop(0, steps)
+    def _(step):
+        columns = pl.ds(pl.multiple_of(step * step_width, step_width), step_width)
+        product[:, columns] = jnp.dot(
+            rows[...], wq[:, columns], preferred_element_type=jnp.float32
+        ).astype(jnp.bfloat16)
+
+    product[:, query_columns:] = jnp.dot(
+        rows[...], wkv[...], preferred_element_type=jnp.float32
+    ).astype(jnp.bfloat16)
+
+    def slot_rows(index):
+        return pl.ds(pl.multiple_of(index * MOST_TREE_NODES, MOST_TREE_NODES), MOST_TREE_NODES)
+
+    def produce(index):
+        blocks[slot_rows(index), :] = jnp.dot(
+            pick_ref[slot_rows(index), :], product[...], preferred_element_type=jnp.float32
+        ).astype(jnp.bfloat16)
+
+    def finish(total):
+        query_ref[...] = total[:, :query_columns]
+        kv_ref[me] = total[:, query_columns:]
+
+    sum_scatter(
+        "req",
+        req_inner,
+        produce,
+        lambda index: blocks.at[slot_rows(index)],
+        near,
+        staged,
+        far,
+        sum_send,
+        sum_recv,
+        finish,
+    )
+    own_kv = kv_ref.at[me]
+    started = start_gather(
+        "tensor", tensor_count, own_kv, lambda index: kv_ref.at[index], kv_send, kv_recv
+    )
+    finish_gather(
+        "tensor", tensor_count, own_kv, lambda index: kv_ref.at[index], kv_send, kv_recv, started
+    )
+    own_cache.wait()
+    for step in range(1, tensor_count):
+        owner = lax.rem(me - step + tensor_count, tensor_count)
+        source, landing = cache_part(owner, me)
+        remote(source, landing, cache_send, cache_recv, step, "tensor", owner).wait_recv()
+    for copy in cache_copies:
+        copy.wait_send()
+
+
+def project(hidden, pick, w_query, keyvalue_weight, cache):
+    tensor_count, req_count = lax.axis_size("tensor"), lax.axis_size("req")
+    req_inner, core_inner = inner_of(req_count), 2
+    rows_here, width = hidden.shape
+    query_columns, kv_columns = w_query.shape[1], keyvalue_weight.shape[1]
+    both = query_columns + kv_columns
+    outer = req_count // req_inner
+    bf16, dma = jnp.bfloat16, pltpu.SemaphoreType.DMA
+    any_space, vmem = pl.BlockSpec(memory_space=pl.ANY), pl.BlockSpec(memory_space=pltpu.VMEM)
+    return pl.pallas_call(
+        functools.partial(
+            project_kernel, req_inner, core_inner, QUERY_HEADS // KEYVALUE_HEADS
+        ),
+        out_shape=(
+            jax.ShapeDtypeStruct((MOST_TREE_NODES, query_columns), bf16),
+            jax.ShapeDtypeStruct((tensor_count, MOST_TREE_NODES, kv_columns), bf16),
+            jax.ShapeDtypeStruct((cache.shape[0] * tensor_count, 2 * HEAD_SIZE), bf16),
+        ),
+        in_specs=[vmem, vmem, any_space, any_space, any_space],
+        out_specs=(vmem, vmem, any_space),
+        scratch_shapes=[
+            pltpu.VMEM((rows_here * tensor_count, width), bf16),
+            pltpu.VMEM(w_query.shape, bf16),
+            pltpu.VMEM(keyvalue_weight.shape, bf16),
+            pltpu.VMEM((rows_here * tensor_count, both), bf16),
+            pltpu.VMEM((req_count * MOST_TREE_NODES, both), bf16),
+            pltpu.VMEM(((req_inner - 1) * outer, MOST_TREE_NODES, both), bf16),
+            pltpu.VMEM((outer - 1, MOST_TREE_NODES, both), bf16),
+            pltpu.VMEM((outer - 1, MOST_TREE_NODES, both), bf16),
+            dma((3,)),
+            dma((tensor_count,)),
+            dma((tensor_count,)),
+            dma((tensor_count,)),
+            dma((tensor_count,)),
+            dma((req_count,)),
+            dma((req_count,)),
+            dma((tensor_count,)),
+            dma((tensor_count,)),
+        ],
+        compiler_params=pltpu.CompilerParams(
+            collective_id=0, has_side_effects=True, vmem_limit_bytes=VMEM_BYTES
+        ),
+    )(hidden, pick, w_query, keyvalue_weight, cache)
+
+
+def output_kernel(
+    req_inner,
+    core_inner,
+    mix_ref,
+    pick_ref,
+    wo_ref,
+    out_ref,
+    wo,
+    slots,
+    rows,
+    product,
+    near,
+    staged,
+    far,
+    load_sem,
+    slot_send,
+    slot_recv,
+    sum_send,
+    sum_recv,
+):
+    me = lax.axis_index("req")
+    rows_here = out_ref.shape[0]
+    load = pltpu.make_async_copy(wo_ref, wo, load_sem.at[0])
+    load.start()
+    greet([("req", req_inner), ("tensor", core_inner)])
+
+    def slot_rows(index):
+        return pl.ds(pl.multiple_of(index * MOST_TREE_NODES, MOST_TREE_NODES), MOST_TREE_NODES)
+
+    def slot_part(index):
+        return slots.at[slot_rows(index)]
+
+    started = start_gather("req", req_inner, mix_ref, slot_part, slot_send, slot_recv)
+    slots[slot_rows(me), :] = mix_ref[...]
+    finish_gather("req", req_inner, mix_ref, slot_part, slot_send, slot_recv, started)
+    steps, step_width = tiles(slots.shape[1])
+
+    @pl.loop(0, steps)
+    def _(step):
+        columns = pl.ds(pl.multiple_of(step * step_width, step_width), step_width)
+        rows[:, columns] = jnp.dot(
+            pick_ref[...], slots[:, columns], preferred_element_type=jnp.float32
+        ).astype(jnp.bfloat16)
+
+    load.wait()
+    out_steps, out_width = tiles(wo.shape[1])
+
+    @pl.loop(0, out_steps)
+    def _(step):
+        columns = pl.ds(pl.multiple_of(step * out_width, out_width), out_width)
+        product[:, columns] = jnp.dot(
+            rows[...], wo[:, columns], preferred_element_type=jnp.float32
+        ).astype(jnp.bfloat16)
+
+    def finish(total):
+        out_ref[...] = total
+
+    sum_scatter(
+        "tensor",
+        core_inner,
+        lambda index: None,
+        lambda index: product.at[
+            pl.ds(pl.multiple_of(index * rows_here, rows_here), rows_here)
+        ],
+        near,
+        staged,
+        far,
+        sum_send,
+        sum_recv,
+        finish,
+    )
+
+
+def output(mix, pick, w_out):
+    tensor_count, req_count = lax.axis_size("tensor"), lax.axis_size("req")
+    req_inner, core_inner = inner_of(req_count), 2
+    outer = tensor_count // core_inner
+    row_total = pick.shape[0]
+    rows_here = row_total // tensor_count
+    depth, width = w_out.shape
+    bf16, dma = jnp.bfloat16, pltpu.SemaphoreType.DMA
+    any_space, vmem = pl.BlockSpec(memory_space=pl.ANY), pl.BlockSpec(memory_space=pltpu.VMEM)
+    return pl.pallas_call(
+        functools.partial(output_kernel, req_inner, core_inner),
+        out_shape=jax.ShapeDtypeStruct((rows_here, width), bf16),
+        in_specs=[vmem, vmem, any_space],
+        out_specs=vmem,
+        scratch_shapes=[
+            pltpu.VMEM(w_out.shape, bf16),
+            pltpu.VMEM((req_count * MOST_TREE_NODES, depth), bf16),
+            pltpu.VMEM((row_total, depth), bf16),
+            pltpu.VMEM((row_total, width), bf16),
+            pltpu.VMEM(((core_inner - 1) * outer, rows_here, width), bf16),
+            pltpu.VMEM((outer - 1, rows_here, width), bf16),
+            pltpu.VMEM((outer - 1, rows_here, width), bf16),
+            dma((1,)),
+            dma((req_count,)),
+            dma((req_count,)),
+            dma((tensor_count,)),
+            dma((tensor_count,)),
+        ],
+        compiler_params=pltpu.CompilerParams(
+            collective_id=1, has_side_effects=True, vmem_limit_bytes=VMEM_BYTES
+        ),
+    )(mix, pick, w_out)
 
 
 def body(
@@ -77,24 +494,18 @@
     home_slot = jnp.sum(
         jnp.where(slot_request[None, :] == request_ids[:, None], request_ids[None, :], 0), axis=1
     )
-    features = lax.all_gather(hidden, "tensor", axis=0, tiled=True)
-    w_both = jnp.concatenate([w_query, keyvalue_weight], axis=1)
     slot_ids = jnp.arange(resident_slots * lax.axis_size("req"), dtype=jnp.int32)
     owner_req = lookup(slot_request, slot_ids // MOST_TREE_NODES)
     node_ids = slot_ids % MOST_TREE_NODES
     is_valid = node_ids < lookup(tree_size, owner_req)
     row_ids = jnp.minimum(lookup(starts, owner_req) + node_ids, row_total - 1)
-    row_ids, is_valid = (row_ids, is_valid)
-    occupied_rows = jnp.take(features, row_ids, axis=0)
-    occupied_rows = jnp.where(is_valid[:, None], occupied_rows, jnp.zeros_like(occupied_rows))
-    projected = lax.psum_scatter(
-        jnp.dot(occupied_rows, w_both, preferred_element_type=jnp.float32).astype(jnp.bfloat16),
-        "req",
-        scatter_dimension=0,
-        tiled=True,
-    )
-    query_here = projected[:, :query_columns]
-    keyval_here = projected[:, query_columns:]
+    all_rows = jnp.arange(row_total, dtype=jnp.int32)
+    pick_rows = (
+        (row_ids[:, None] == all_rows[None, :]) & is_valid[:, None]
+    ).astype(jnp.bfloat16)
+    query_here, keyval_parts, head_cache = project(
+        hidden, pick_rows, w_query, keyvalue_weight, keyvalue_cache[0]
+    )
     my_requests = lax.dynamic_slice_in_dim(
         slot_request, req_index * resident_requests, resident_requests
     )
@@ -108,21 +519,17 @@
     tree_depth = jnp.sum(closure, axis=-1) - 1.0
     cosine_table, sine_table = rotary(tree_depth.reshape(resident_slots))
     tree_ok = (closure > 0.5)[:, :, None, :]
-    keyvalue_every_head = lax.all_gather(keyval_here, "tensor", axis=1, tiled=True)
+    keyvalue_every_head = jnp.transpose(keyval_parts, (1, 0, 2))
     query_mine = rotate(
         query_here.reshape(resident_slots, heads_here, HEAD_SIZE), cosine_table, sine_table
     ).astype(jnp.bfloat16)
     query_grid = query_mine.reshape(resident_requests, MOST_TREE_NODES, heads_here, HEAD_SIZE)
-    cache_portion = lax.all_gather(keyvalue_cache, "tensor", axis=1, tiled=True)
-    portion_length = cache_portion.shape[1]
-    portion_rows = cache_portion.reshape(
-        resident_requests, portion_length, KEYVALUE_HEADS, 2, HEAD_SIZE
-    )
-    head_rows = lax.dynamic_index_in_dim(portion_rows, kv_head, axis=2, keepdims=False)
+    cache_keys = head_cache[None, :, :HEAD_SIZE]
+    cache_values = head_cache[None, :, HEAD_SIZE:]
     top_now = jnp.full((resident_requests, MOST_TREE_NODES, heads_here), NEGATIVE, jnp.float32)
     scores = (
         jnp.einsum(
-            "rkhd,rpd->rkhp", query_grid, head_rows[:, :, 0], preferred_element_type=jnp.float32
+            "rkhd,rpd->rkhp", query_grid, cache_keys, preferred_element_type=jnp.float32
         )
         * score_scale
     )
@@ -133,7 +540,7 @@
     mix_next = jnp.einsum(
         "rkhp,rpd->rkhd",
         weights.astype(jnp.bfloat16),
-        head_rows[:, :, 1],
+        cache_values,
         preferred_element_type=jnp.float32,
     )
     keyvalue_layout = keyvalue_every_head.reshape(resident_slots, 2, HEAD_SIZE, KEYVALUE_HEADS)
@@ -165,17 +572,14 @@
         .astype(jnp.bfloat16)
         .reshape(resident_slots, heads_here * HEAD_SIZE)
     )
-    slot_attention = lax.all_gather(attention, "req", axis=0, tiled=True)
-    row_ids = jnp.arange(row_total // tensor_count * lax.axis_size("tensor"), dtype=jnp.int32)
+    row_ids = all_rows
     owner_req = jnp.sum((row_ends[None, :] <= row_ids[:, None]).astype(jnp.int32), axis=1)
     slot_ids = lookup(home_slot, owner_req) * MOST_TREE_NODES + row_ids - lookup(starts, owner_req)
-    occupied_rows = jnp.take(slot_attention, slot_ids, axis=0)
-    return lax.psum_scatter(
-        jnp.dot(occupied_rows, w_out, preferred_element_type=jnp.float32).astype(jnp.bfloat16),
-        "tensor",
-        scatter_dimension=0,
-        tiled=True,
-    )
+    all_slots = jnp.arange(
+        resident_slots * lax.axis_size("req"), dtype=jnp.int32
+    )
+    pick_slots = (slot_ids[:, None] == all_slots[None, :]).astype(jnp.bfloat16)
+    return output(attention, pick_slots, w_out)
 
 
 def solution(mesh):

time: 219 us -> 114 us (0.52)
  the two profiles are of different devices: /device:TPU:0 before, /device:TPU:25 now
where the time goes in v1:
time: 114 us
  Pallas kernels  89.5 us (79%)
  other arithmetic  12.1 us (11%)
  matrix products  7.4 us (6%)
  local copies, waits for them, and re-layouts  4.59 us (4%)
    pallas_call x1, Pallas kernels, project(): pl.pallas_call(functools.partial(project_kernel, req_inner, core_inner, Q...  46.1 us
    pallas_call x1, Pallas kernels, output(): pl.pallas_call(functools.partial(output_kernel, req_inner, core_inner), o...  43.4 us
    dot_general x1, matrix products, body(): jnp.einsum('rkhd,rpd->rkhp', query_grid, cache_keys, preferred_element_ty...  3.5 us
    reduce_sum x1, other arithmetic, body(): sum_next = jnp.sum(weights, axis=-1)  3.15 us
    unnamed x12, local copies, waits for them, and re-layouts  2.46 us

profile of v1, /device:TPU:25, one launch (start us, length us, event | category | flops | bytes accessed | tf_op | source)
XLA Modules:
  0.0 114.0 jit_solution(8085368810076534342)
XLA Ops:
  0.0 0.0 copy-start.2
  0.0 0.0 copy-start.1
  0.0 0.0 copy-start.3
  0.0 0.8 reduce-window.8
  0.9 0.7 bitcast_subtract_fusion
  1.5 0.7 select_reduce_fusion.4
  2.3 0.7 select_reduce_fusion.2
  3.1 0.8 fusion.18.pick_ref
  3.9 46.1 %shard_map.91 = (bf16[48,2048]{1,0:T(8,128)(2,1)}, bf16[4,48,256]{2,1,0:T(8,128)(2,1)}, bf16[4096,256]{1,0:T(8,128)(2,1)}) custom-call(bf16[48,2048]{1,0:T(8,128)(2,1)} %hidden_ref.1, bf16[384,192]{1,0:T(8,128)(2,1)} %fusion.18.pick_ref, bf16[2048,2048]{1,0:T(8,128)(2,1)} %wq_ref.1, bf16[2048,256]{1,0:T(8,128)(2,1)} %wkv_ref.1, bf16[1024,1024]{1,0:T(8,128)(2,1)} %bitcast.64), custom_call_target="tpu_custom_call" | custom-call | tf_op jit(solution)/shard_map/pallas_call | solution.py:326
  50.0 1.1 copy.15
  51.1 0.1 constant_dynamic-slice_fusion
  51.3 0.1 copy.16
  51.4 0.1 slice_negate_fusion.1
  51.4 0.0 copy-done.2
  51.4 0.6 dynamic_slice.7
  52.0 0.6 iota_compare_fusion.7
  52.7 0.0 copy-done.1
  52.7 0.1 select_reduce_fusion.8
  52.8 0.1 fusion.27
  52.9 0.1 convolution_minimum_fusion.5
  53.1 0.2 convolution_minimum_fusion.4
  53.2 0.2 convolution_minimum_fusion.3
  53.4 0.2 convolution_minimum_fusion.2
  53.5 0.2 convolution_minimum_fusion.1
  53.7 0.3 fusion.48
  54.0 0.1 fusion.34
  54.1 0.2 fusion.31
  54.3 1.0 convert_bitcast_fusion
  55.2 0.1 copy.19
  55.3 0.2 slice_negate_fusion
  55.5 0.2 maximum_multiply_fusion
  55.7 1.2 %fusion.23 = bf16[6,8,16,128]{3,1,2,0:T(8,128)(2,1)S(1)} fusion(f32[6,8,16,128]{3,2,1,0:T(8,128)S(1)} %bitcast.68, f32[6,8,16,128]{3,2,1,0:T(8,128)S(1)} %bitcast.67, bf16[48,2048]{1,0:T(8,128)(2,1)} %get-tuple-element.8), kind=kLoop, calls=%fused_computation.37 | loop fusion | flops 393216 | bytes 1179648
  56.9 0.5 select_reduce_fusion.1
  57.4 0.0 copy-done.3
  57.5 0.1 broadcast_in_dim.161
  57.6 0.1 gt.29
  57.7 0.0 copy-start
  57.7 3.5 %select_reduce_fusion = (f32[48,16]{1,0:T(8,128)S(1)}, f32[48,16,4096]{2,1,0:T(8,128)S(1)}) fusion(pred[4096]{0:T(1024)(128)(4,1)S(1)} %gt.29, bf16[48,16,128]{2,1,0:T(8,128)(2,1)S(1)} %bitcast.66, bf16[4096,256]{1,0:T(8,128)(2,1)} %get-tuple-element.9), kind=kOutput, calls=%fused_computation.1 | convolution fusion | flops 814742784 | bytes 13835264 | tf_op jit(solution)/shard_map/rkhd,rpd->rkhp/dot_general | solution.py:531
  61.2 3.1 %fusion = f32[48,16]{1,0:T(8,128)S(1)} fusion(f32[48,16,4096]{2,1,0:T(8,128)S(1)} %get-tuple-element.32, f32[48,16]{1,0:T(8,128)S(1)} %get-tuple-element.20, pred[4096]{0:T(1024)(128)(4,1)S(1)} %gt.29), kind=kLoop, calls=%fused_computation.2 | loop fusion | flops 12582144 | bytes 12593152 | tf_op jit(solution)/shard_map/reduce_sum | solution.py:539
  64.4 0.3 fusion.19
  64.7 0.0 copy-done
  64.7 2.1 %fusion.6 = f32[48,16,128]{2,1,0:T(8,128)S(1)} fusion(f32[48,16,4096]{2,1,0:T(8,128)S(1)} %get-tuple-element.32, f32[48,16]{1,0:T(8,128)S(1)} %get-tuple-element.20, pred[4096]{0:T(1024)(128)(4,1)S(1)} %gt.29, bf16[4096,256]{1,0:T(8,128)(2,1)S(1)} %copy-done, f32[48,16]{1,0:T(8,128)S(1)} %get-tuple-element.16), kind=kOutput, calls=%fused_computation.9 | convolution fusion | flops 817987584 | bytes 14077952 | tf_op jit(solution)/shard_map/rkhp,rpd->rkhd/dot_general | solution.py:540
  66.8 0.3 fusion.9
  67.2 0.7 copy.30
  67.9 0.1 convert_reduce_fusion
  68.0 0.1 select_reduce_fusion.7
  68.1 0.1 select_reduce_fusion.6
  68.2 0.7 fusion.21.pick_ref
  68.9 43.4 %shard_map.92 = bf16[48,2048]{1,0:T(8,128)(2,1)} custom-call(bf16[48,2048]{1,0:T(8,128)(2,1)} %bitcast.69, bf16[192,384]{1,0:T(8,128)(2,1)} %fusion.21.pick_ref, bf16[2048,2048]{1,0:T(8,128)(2,1)} %wo_ref.1), custom_call_target="tpu_custom_call" | custom-call | tf_op jit(solution)/shard_map/pallas_call | solution.py:444
  112.4 1.6 %copy.32 = bf16[48,2048]{1,0:T(8,128)(2,1)} copy(bf16[48,2048]{1,0:T(8,128)(2,1)} %shard_map.92) | data formatting | bytes 393216
  (13 shorter events, 0.2 us)
Async XLA Ops:
  0.0 51.4 %copy-start.2 = (s32[8]{0:T(128)S(1)}, s32[8]{0:T(128)}, u32[]{:S(2)}) copy-start(s32[8]{0:T(128)} %param.17) | copy-start | bytes 100
  0.0 52.7 %copy-start.1 = (s32[8,48]{1,0:T(8,128)S(1)}, s32[8,48]{1,0:T(8,128)}, u32[]{:S(2)}) copy-start(s32[8,48]{1,0:T(8,128)} %param.16) | copy-start | bytes 4612
  0.0 57.4 %copy-start.3 = (s32[1,256]{1,0:T(1,128)S(1)}, s32[1,256]{1,0:T(1,128)}, u32[]{:S(2)}) copy-start(s32[1,256]{1,0:T(1,128)} %param.14) | copy-start | bytes 3076
  57.7 7.0 %copy-start = (bf16[4096,256]{1,0:T(8,128)(2,1)S(1)}, bf16[4096,256]{1,0:T(8,128)(2,1)}, u32[]{:S(2)}) copy-start(bf16[4096,256]{1,0:T(8,128)(2,1)} %get-tuple-element.9) | copy-start | bytes 6291460

commit v2 on v0

v2 whole, which is shorter than its diff:
```python
import functools
import math

import jax
import jax.numpy as jnp
from jax import lax
from jax.experimental import pallas as pl
from jax.experimental.pallas import tpu as pltpu
from jax.sharding import PartitionSpec as P

HEAD_SIZE = 128
QUERY_HEADS = 64
KEYVALUE_HEADS = 4
MOST_TREE_NODES = 48
CACHE_POSITIONS = 4096
CBLK = 16


ROPE_BASE = 500000.0
NEGATIVE = -1e30


def lookup(table_vals, index_vals):
    table_ids = jnp.arange(table_vals.shape[0], dtype=jnp.int32)
    return jnp.sum(
        jnp.where(index_vals[:, None] == table_ids[None, :], table_vals[None, :], 0), axis=1
    )


def ancestors(parents):
    node_ids = jnp.arange(MOST_TREE_NODES, dtype=jnp.int32)
    linked = (parents[..., :, None] == node_ids).astype(jnp.float32)
    identity = (node_ids[:, None] == node_ids[None, :]).astype(jnp.float32)
    closure = jnp.maximum(linked, identity)
    for sweep in range((MOST_TREE_NODES - 1).bit_length()):
        closure = jnp.minimum(jnp.matmul(closure, closure, precision=lax.Precision.HIGHEST), 1.0)
    return closure


def rotary(tree_depth):
    half_ids = jnp.arange(HEAD_SIZE // 2, dtype=jnp.float32)
    inv_freq = 1.0 / ROPE_BASE ** (half_ids * 2.0 / HEAD_SIZE)
    angles = (tree_depth + CACHE_POSITIONS)[..., None] * inv_freq
    angles = jnp.concatenate([angles, angles], axis=-1)
    return (jnp.cos(angles), jnp.sin(angles))


MESH = pl.DeviceIdType.MESH
VMEM_BYTES = 56 * 1024 * 1024


def inner_of(count):
    inner = 1
    while inner * inner * 4 <= count:
        inner *= 2
    return inner


def target(axis, index):
    other = "tensor" if axis == "req" else "req"
    return {axis: index, other: lax.axis_index(other)}


def place(axis, inner):
    count = lax.axis_size(axis)
    me = lax.axis_index(axis)
    outer = count // inner
    major, minor = me // inner, lax.rem(me, inner)

    def at(step_major, step_minor):
        return lax.rem(major + step_major + outer, outer) * inner + lax.rem(
            minor + step_minor + inner, inner
        )

    return outer, at


def greet(axes):
    barrier = pltpu.get_barrier_semaphore()
    greeted = 0
    for axis, inner in axes:
        outer, at = place(axis, inner)
        steps = [(d, 0) for d in range(1, outer)] + [(0, e) for e in range(1, inner)]
        for d, e in steps:
            pl.semaphore_signal(
                barrier, inc=1, device_id=target(axis, at(d, e)), device_id_type=MESH
            )
            greeted += 1
    pl.semaphore_wait(barrier, greeted)


def remote(source, landing, sems, slot, axis, index):
    return pltpu.make_async_remote_copy(
        src_ref=source,
        dst_ref=landing,
        send_sem=sems[0].at[slot],
        recv_sem=sems[1].at[slot],
        device_id=target(axis, index),
        device_id_type=MESH,
    )


class Gather:
    def __init__(self, axis, inner, part, sems, base=0):
        self.axis, self.inner, self.part, self.sems, self.base = axis, inner, part, sems, base
        self.outer, self.at = place(axis, inner)
        self.started = []

    def copy(self, block, d, e, index):
        return remote(block, block, self.sems, self.base + e * self.outer + d, self.axis, index)

    def start(self):
        own = self.part(self.at(0, 0))
        for d in range(1, self.outer):
            self.started.append(self.copy(own, d, 0, self.at(d, 0)))
            self.started[-1].start()
        for e in range(1, self.inner):
            self.started.append(self.copy(own, 0, e, self.at(0, e)))
            self.started[-1].start()

    def forward(self):
        for d in range(1, self.outer):
            landed = self.part(self.at(-d, 0))
            self.copy(landed, d, 0, self.at(d, 0)).wait_recv()
            for e in range(1, self.inner):
                self.started.append(self.copy(landed, d, e, self.at(0, e)))
                self.started[-1].start()

    def finish(self):
        for e in range(1, self.inner):
            for d in range(self.outer):
                self.copy(self.part(self.at(-d, -e)), d, e, self.at(0, e)).wait_recv()

    def drain(self):
        for copy in self.started:
            copy.wait_send()


class SumScatter:
    def __init__(self, axis, inner, part, near, staged, far, sems, base=0):
        self.axis, self.inner, self.part = axis, inner, part
        self.near, self.staged, self.far = near, staged, far
        self.sems, self.base = sems, base
        self.outer, self.at = place(axis, inner)
        self.order = list(range(1, self.outer)) + [0]
        self.started = []

    def near_copy(self, d, e):
        return remote(
            self.part(self.at(d, e)),
            self.near.at[(e - 1) * self.outer + d],
            self.sems,
            self.base + e * self.outer + d,
            self.axis,
            self.at(0, e),
        )

    def far_copy(self, d):
        return remote(
            self.staged.at[d - 1],
            self.far.at[d - 1],
            self.sems,
            self.base + d,
            self.axis,
            self.at(d, 0),
        )

    def start(self, produce):
        for d in self.order:
            for e in range(1, self.inner):
                produce(self.at(d, e))
                self.started.append(self.near_copy(d, e))
                self.started[-1].start()
        for d in self.order:
            produce(self.at(d, 0))

    def forward(self):
        for d in self.order:
            total = self.part(self.at(d, 0))[...].astype(jnp.float32)
            for e in range(1, self.inner):
                self.near_copy(d, e).wait_recv()
                total = total + self.near[(e - 1) * self.outer + d].astype(jnp.float32)
            if d:
                self.staged[d - 1] = total.astype(jnp.bfloat16)
                self.started.append(self.far_copy(d))
                self.started[-1].start()
        self.total = total

    def finish(self):
        total = self.total
        for d in range(1, self.outer):
            self.far_copy(d).wait_recv()
            total = total + self.far[d - 1].astype(jnp.float32)
        return total.astype(jnp.bfloat16)

    def drain(self):
        for copy in self.started:
            copy.wait_send()


def tiles(width):
    step = 256 if width % 256 == 0 else width
    return width // step, step


CHUNK_HEADS = 4
OUT_PARTS = 2


def kernel(
    req_inner,
    core_inner,
    chunks,
    hidden_ref,
    pick_ref,
    unpick_ref,
    cosine_ref,
    sine_ref,
    tree_ref,
    live_ref,
    wq_ref,
    wkv_ref,
    cache_ref,
    wo_ref,
    out_ref,
    rows,
    wq,
    wkv,
    wo,
    cache,
    kv_all,
    slots,
    mixed_rows,
    load_sem,
    row_send,
    row_recv,
    cache_send,
    cache_recv,
    sum_send,
    sum_recv,
    kv_send,
    kv_recv,
    slot_send,
    slot_recv,
    out_send,
    out_recv,
    *buffers,
):
    tensor_count, req_count = lax.axis_size("tensor"), lax.axis_size("req")
    me, slot = lax.axis_index("tensor"), lax.axis_index("req")
    rows_here = hidden_ref.shape[0]
    query_columns = wq.shape[1]
    heads_here = query_columns // HEAD_SIZE
    group_size = QUERY_HEADS // KEYVALUE_HEADS
    pair = 2 * HEAD_SIZE
    positions = cache_ref.shape[0]
    chunk_width = query_columns // chunks
    chunk_heads = chunk_width // HEAD_SIZE
    score_scale = 1.0 / math.sqrt(HEAD_SIZE)
    loads = [
        pltpu.make_async_copy(source, landing, load_sem.at[i])
        for i, (source, landing) in enumerate(((wkv_ref, wkv), (wq_ref, wq), (wo_ref, wo)))
    ]
    for load in loads:
        load.start()
    greet([("tensor", tensor_count), ("req", req_inner)])

    def row_span(index):
        return pl.ds(pl.multiple_of(index * rows_here, rows_here), rows_here)

    def slot_span(index):
        return pl.ds(pl.multiple_of(index * MOST_TREE_NODES, MOST_TREE_NODES), MOST_TREE_NODES)

    rows[row_span(me), :] = hidden_ref[...]
    row_gather = Gather(
        "tensor", core_inner, lambda index: rows.at[row_span(index)], (row_send, row_recv)
    )
    row_gather.start()
    row_gather.forward()
    row_gather.finish()

    def cache_part(owner, reader):
        head = reader * heads_here // group_size
        return (
            cache_ref.at[:, pl.ds(pl.multiple_of(head * pair, pair), pair)],
            cache.at[pl.ds(pl.multiple_of(owner * positions, positions), positions)],
        )

    own_cache = pltpu.make_async_copy(*cache_part(me, me), load_sem.at[3])
    own_cache.start()
    cache_sems = (cache_send, cache_recv)
    cache_copies = []
    for step in range(1, tensor_count):
        reader = lax.rem(me + step, tensor_count)
        copy = remote(*cache_part(me, reader), cache_sems, step, "tensor", reader)
        copy.start()
        cache_copies.append(copy)

    scatters = []
    for c in range(chunks + 1):
        product, blocks, near, staged, far = buffers[5 * c : 5 * c + 5]
        if c == 0:
            loads[0].wait()
            product[...] = jnp.dot(
                rows[...], wkv[...], preferred_element_type=jnp.float32
            ).astype(jnp.bfloat16)
        else:
            if c == 1:
                loads[1].wait()
            product[...] = jnp.dot(
                rows[...],
                wq[:, (c - 1) * chunk_width : c * chunk_width],
                preferred_element_type=jnp.float32,
            ).astype(jnp.bfloat16)

        def produce(index, blocks=blocks, product=product):
            blocks[slot_span(index), :] = jnp.dot(
                pick_ref[slot_span(index), :], product[...], preferred_element_type=jnp.float32
            ).astype(jnp.bfloat16)

        scatter = SumScatter(
            "req",
            req_inner,
            lambda index, blocks=blocks: blocks.at[slot_span(index)],
            near,
            staged,
            far,
            (sum_send, sum_recv),
            c * req_count,
        )
        scatter.start(produce)
        scatters.append(scatter)

    scatters[0].forward()
    scatters[1].forward()
    kv_all[me] = scatters[0].finish()
    kv_gather = Gather(
        "tensor", tensor_count, lambda index: kv_all.at[index], (kv_send, kv_recv)
    )
    kv_gather.start()
    cosine, sine = cosine_ref[...], sine_ref[...]

    def rotated(values):
        widened = values.astype(jnp.float32)
        turned = jnp.concatenate(
            [widened[:, HEAD_SIZE // 2 :], widened[:, : HEAD_SIZE // 2]], axis=1
        )
        return (widened * cosine + turned * sine).astype(jnp.bfloat16)

    kv_gather.finish()
    kv_head = me * heads_here // group_size
    kv_columns = kv_all.shape[2]
    source_ids = lax.broadcasted_iota(jnp.int32, (kv_columns, pair), 0)
    wanted_ids = lax.broadcasted_iota(jnp.int32, (kv_columns, pair), 1) * KEYVALUE_HEADS + kv_head
    head_kv = jnp.zeros((MOST_TREE_NODES, pair), jnp.float32)
    for t in range(tensor_count):
        chosen = jnp.where(source_ids + t * kv_columns == wanted_ids, 1.0, 0.0)
        head_kv = head_kv + jnp.dot(
            kv_all[t], chosen.astype(jnp.bfloat16), preferred_element_type=jnp.float32
        )
    tree_key = rotated(head_kv[:, :HEAD_SIZE])
    tree_value = head_kv[:, HEAD_SIZE:].astype(jnp.bfloat16)
    own_cache.wait()
    for step in range(1, tensor_count):
        owner = lax.rem(me - step + tensor_count, tensor_count)
        remote(*cache_part(owner, me), cache_sems, step, "tensor", owner).wait_recv()

    def scored(query, key):
        return (
            lax.dot_general(
                query, key, (((1,), (1,)), ((), ())), preferred_element_type=jnp.float32
            )
            * score_scale
        )

    tile = 1024
    gathers = []
    for c in range(chunks):
        if c + 1 < chunks:
            scatters[c + 2].forward()
        found = scatters[c + 1].finish()
        query = jnp.concatenate(
            [rotated(found[:, h * HEAD_SIZE : (h + 1) * HEAD_SIZE]) for h in range(chunk_heads)],
            axis=0,
        )
        scores = scored(query, tree_key) + tree_ref[...]
        top = jnp.max(scores, axis=1, keepdims=True)
        weights = jnp.exp(scores - top)
        total = jnp.sum(weights, axis=1, keepdims=True)
        mix = jnp.dot(
            weights.astype(jnp.bfloat16), tree_value, preferred_element_type=jnp.float32
        )

        def step_tile(i, carry, query=query):
            top, total, mix = carry
            span = pl.ds(pl.multiple_of(i * tile, tile), tile)
            scores = scored(query, cache[span, :HEAD_SIZE]) + live_ref[:, span]
            higher = jnp.maximum(top, jnp.max(scores, axis=1, keepdims=True))
            scale = jnp.exp(top - higher)
            weights = jnp.exp(scores - higher)
            total = total * scale + jnp.sum(weights, axis=1, keepdims=True)
            mix = mix * scale + jnp.dot(
                weights.astype(jnp.bfloat16),
                cache[span, HEAD_SIZE:],
                preferred_element_type=jnp.float32,
            )
            return higher, total, mix

        top, total, mix = lax.fori_loop(
            0, cache.shape[0] // tile, step_tile, (top, total, mix)
        )
        mix = (mix / total).astype(jnp.bfloat16)
        for h in range(chunk_heads):
            low = c * chunk_width + h * HEAD_SIZE
            slots[slot_span(slot), low : low + HEAD_SIZE] = mix[
                h * MOST_TREE_NODES : (h + 1) * MOST_TREE_NODES
            ]
        gather = Gather(
            "req",
            req_inner,
            lambda index, c=c: slots.at[
                slot_span(index), c * chunk_width : (c + 1) * chunk_width
            ],
            (slot_send, slot_recv),
            c * req_count,
        )
        gather.start()
        if gathers:
            gathers[-1].forward()
        gathers.append(gather)
    gathers[-1].forward()
    for c, gather in enumerate(gathers):
        gather.finish()
        columns = slice(c * chunk_width, (c + 1) * chunk_width)
        mixed_rows[:, columns] = jnp.dot(
            unpick_ref[...], slots[:, columns], preferred_element_type=jnp.float32
        ).astype(jnp.bfloat16)

    loads[2].wait()
    out_width = wo.shape[1] // OUT_PARTS
    out_sums = []
    for p in range(OUT_PARTS):
        product, near, staged, far = buffers[5 * (chunks + 1) + 4 * p :][:4]
        steps, step_width = tiles(out_width)

        @pl.loop(0, steps)
        def _(step, p=p, product=product):
            columns = pl.ds(pl.multiple_of(step * step_width, step_width), step_width)
            wide = pl.ds(
                pl.multiple_of(p * out_width + step * step_width, step_width), step_width
            )
            product[:, columns] = jnp.dot(
                mixed_rows[...], wo[:, wide], preferred_element_type=jnp.float32
            ).astype(jnp.bfloat16)

        out_sum = SumScatter(
            "tensor",
            core_inner,
            lambda index, product=product: product.at[row_span(index)],
            near,
            staged,
            far,
            (out_send, out_recv),
            p * tensor_count,
        )
        out_sum.start(lambda index: None)
        out_sums.append(out_sum)
    for out_sum in out_sums:
        out_sum.forward()
    for p, out_sum in enumerate(out_sums):
        out_ref[:, p * out_width : (p + 1) * out_width] = out_sum.finish()
    for work in [row_gather, kv_gather] + scatters + gathers + out_sums:
        work.drain()
    for copy in cache_copies:
        copy.wait_send()


def run(hidden, tables, w_query, keyvalue_weight, cache, w_out):
    tensor_count, req_count = lax.axis_size("tensor"), lax.axis_size("req")
    req_inner, core_inner = inner_of(req_count), 2
    rows_here, width = hidden.shape
    row_total = rows_here * tensor_count
    query_columns, kv_columns = w_query.shape[1], keyvalue_weight.shape[1]
    chunks = query_columns // HEAD_SIZE // CHUNK_HEADS
    depth, out_columns = w_out.shape
    bf16, dma = jnp.bfloat16, pltpu.SemaphoreType.DMA
    any_space, vmem = pl.BlockSpec(memory_space=pl.ANY), pl.BlockSpec(memory_space=pltpu.VMEM)
    outer, core_outer = req_count // req_inner, tensor_count // core_inner
    buffers = []
    for columns in [kv_columns] + [query_columns // chunks] * chunks:
        buffers += [
            pltpu.VMEM((row_total, columns), bf16),
            pltpu.VMEM((req_count * MOST_TREE_NODES, columns), bf16),
            pltpu.VMEM(((req_inner - 1) * outer, MOST_TREE_NODES, columns), bf16),
            pltpu.VMEM((outer - 1, MOST_TREE_NODES, columns), bf16),
            pltpu.VMEM((outer - 1, MOST_TREE_NODES, columns), bf16),
        ]
    for part in range(OUT_PARTS):
        columns = out_columns // OUT_PARTS
        buffers += [
            pltpu.VMEM((row_total, columns), bf16),
            pltpu.VMEM(((core_inner - 1) * core_outer, rows_here, columns), bf16),
            pltpu.VMEM((core_outer - 1, rows_here, columns), bf16),
            pltpu.VMEM((core_outer - 1, rows_here, columns), bf16),
        ]
    sems = [tensor_count, tensor_count, (chunks + 1) * req_count, tensor_count]
    sems += [chunks * req_count, OUT_PARTS * tensor_count]
    return pl.pallas_call(
        functools.partial(kernel, req_inner, core_inner, chunks),
        out_shape=jax.ShapeDtypeStruct((rows_here, out_columns), bf16),
        in_specs=[vmem] * 7 + [any_space] * 4,
        out_specs=vmem,
        scratch_shapes=[
            pltpu.VMEM((row_total, width), bf16),
            pltpu.VMEM(w_query.shape, bf16),
            pltpu.VMEM(keyvalue_weight.shape, bf16),
            pltpu.VMEM(w_out.shape, bf16),
            pltpu.VMEM((cache.shape[0] * tensor_count, 2 * HEAD_SIZE), bf16),
            pltpu.VMEM((tensor_count, MOST_TREE_NODES, kv_columns), bf16),
            pltpu.VMEM((req_count * MOST_TREE_NODES, depth), bf16),
            pltpu.VMEM((row_total, depth), bf16),
            dma((4,)),
        ]
        + [dma((count,)) for count in sems for both in range(2)]
        + buffers,
        compiler_params=pltpu.CompilerParams(
            collective_id=0, has_side_effects=True, vmem_limit_bytes=VMEM_BYTES
        ),
    )(hidden, *tables, w_query, keyvalue_weight, cache, w_out)


def body(
    hidden,
    w_query,
    keyvalue_weight,
    w_out,
    keyvalue_cache,
    cache_live,
    tree_size,
    tree_parent,
    slot_request,
):
    tensor_count = lax.axis_size("tensor")
    req_index = lax.axis_index("req")
    resident_requests = keyvalue_cache.shape[0]
    resident_slots = resident_requests * MOST_TREE_NODES
    row_total = hidden.shape[0] * tensor_count
    row_ends = jnp.cumsum(tree_size)
    starts = row_ends - tree_size
    request_ids = jnp.arange(tree_size.shape[0], dtype=jnp.int32)
    home_slot = jnp.sum(
        jnp.where(slot_request[None, :] == request_ids[:, None], request_ids[None, :], 0), axis=1
    )
    slot_ids = jnp.arange(resident_slots * lax.axis_size("req"), dtype=jnp.int32)
    owner_req = lookup(slot_request, slot_ids // MOST_TREE_NODES)
    node_ids = slot_ids % MOST_TREE_NODES
    is_valid = node_ids < lookup(tree_size, owner_req)
    row_ids = jnp.minimum(lookup(starts, owner_req) + node_ids, row_total - 1)
    all_rows = jnp.arange(row_total, dtype=jnp.int32)
    pick_rows = (
        (row_ids[:, None] == all_rows[None, :]) & is_valid[:, None]
    ).astype(jnp.bfloat16)
    my_requests = lax.dynamic_slice_in_dim(
        slot_request, req_index * resident_requests, resident_requests
    )
    parents = jnp.sum(
        jnp.where(
            my_requests[:, None, None] == request_ids[None, :, None], tree_parent[None, :, :], 0
        ),
        axis=1,
    )
    closure = ancestors(parents)
    tree_depth = jnp.sum(closure, axis=-1) - 1.0
    cosine_table, sine_table = rotary(tree_depth.reshape(resident_slots))
    signed_sine = sine_table * jnp.where(jnp.arange(HEAD_SIZE) < HEAD_SIZE // 2, -1.0, 1.0)
    tree_bias = jnp.tile(jnp.where(closure[0] > 0.5, 0.0, NEGATIVE), (CHUNK_HEADS, 1))
    live_bias = jnp.where(jnp.repeat(cache_live, CBLK, axis=1) > 0, 0.0, NEGATIVE)
    row_ids = all_rows
    owner_req = jnp.sum((row_ends[None, :] <= row_ids[:, None]).astype(jnp.int32), axis=1)
    slot_ids = lookup(home_slot, owner_req) * MOST_TREE_NODES + row_ids - lookup(starts, owner_req)
    all_slots = jnp.arange(
        resident_slots * lax.axis_size("req"), dtype=jnp.int32
    )
    pick_slots = (slot_ids[:, None] == all_slots[None, :]).astype(jnp.bfloat16)
    tables = (pick_rows, pick_slots, cosine_table, signed_sine, tree_bias, live_bias)
    return run(hidden, tables, w_query, keyvalue_weight, keyvalue_cache[0], w_out)


def solution(mesh):
    placed = (
        P("tensor", "req"),
        P("req", "tensor"),
        P("req", "tensor"),
        P("tensor", "req"),
        P("req", "tensor", None),
        P("req", None),
        P(),
        P(),
        P(),
    )
    return jax.shard_map(
        body, mesh=mesh, in_specs=placed, out_specs=P("tensor", "req"), check_vma=False
    )
```

time: 219 us -> 101 us (0.46)
  waiting for transfers between devices: 129 us -> 0 us
  Pallas kernels: 0 us -> 86.7 us
  local copies, waits for them, and re-layouts: 26.6 us -> 4.31 us
  matrix products: 20.9 us -> 1.02 us
  blocking collectives: 15.8 us -> 0 us
  between operations: 15.2 us -> 0.11 us
    pallas_call x0 -> x1, Pallas kernels: none -> 86.7 us  [run(): pl.pallas_call(functools.partial(kernel, req_inner, core_inner, chunks),...]
    reduce_scatter x2 -> x0, waiting for transfers between devices: 85.4 us -> none  [the longest x1 63.3 us: body(): lax.psum_scatter(jnp.dot(occupied_rows, w_both, preferred_element_type=jn...]
    all_gather x2 -> x0, waiting for transfers between devices: 42.9 us -> none  [the longest x1 42.9 us: body(): slot_attention = lax.all_gather(attention, 'req', axis=0, tiled=True)]
    dot_general x6 -> x0, matrix products: 19.9 us -> none  [the longest x1 8.63 us: body(): jnp.dot(occupied_rows, w_both, preferred_element_type=jnp.float32)]
    all_gather x2 -> x0, blocking collectives: 15.8 us -> none  [the longest x1 10.3 us: body(): features = lax.all_gather(hidden, 'tensor', axis=0, tiled=True)]
    reshape x1 -> x0, local copies, waits for them, and re-layouts: 14.3 us -> none  [body(): cache_portion.reshape(resident_requests, portion_length, KEYVALUE_HEADS,...]
    gather x2 -> x0, local copies, waits for them, and re-layouts: 5.96 us -> none  [the longest x1 3.51 us: body(): occupied_rows = jnp.take(slot_attention, slot_ids, axis=0)]
    dynamic_slice x3 -> x0, local copies, waits for them, and re-layouts: 3.48 us -> none  [the longest x1 3.24 us: body(): lax.dynamic_index_in_dim(portion_rows, kv_head, axis=2, keepdims=False)]
  transfers between devices with their start and end apart: 4 -> 0, of which waited for: 3 -> 0; matrix products, arithmetic and copies ran while one was open for 3% -> 0% of each run, Pallas kernels for 0% -> 0%
where the time goes in v2:
time: 101 us
  Pallas kernels  86.7 us (86%)
  other arithmetic  8.66 us (9%)
  local copies, waits for them, and re-layouts  4.31 us (4%)
  matrix products  1.02 us (1%)
    pallas_call x1, Pallas kernels, run(): pl.pallas_call(functools.partial(kernel, req_inner, core_inner, chunks),...  86.7 us

profile of v2, /device:TPU:0, one launch (start us, length us, event | category | flops | bytes accessed | tf_op | source)
XLA Modules:
  0.0 100.8 jit_solution(6543435259325806087)
XLA Ops:
  0.0 1.2 %dynamic_slice.3 = s32[1]{0:T(128)} dynamic-slice(s32[8]{0:T(128)} %param.17, s32[]{:T(128)S(6)} %select_n.84), dynamic_slice_sizes={1} | dynamic-slice | bytes 12 | tf_op jit(solution)/shard_map/dynamic_slice | solution.py:563
  1.2 0.6 iota_compare_fusion.7
  1.9 0.8 select_reduce_fusion.5
  2.7 0.8 reduce-window.8
  3.5 0.7 bitcast_subtract_fusion
  4.2 0.8 select_reduce_fusion.6
  4.9 0.1 convert_reduce_fusion
  5.0 0.1 select_reduce_fusion.4
  5.1 0.7 compare_select_fusion.1
  5.8 0.7 select_reduce_fusion.2
  6.6 0.7 select_reduce_fusion
  7.3 0.1 fusion.3
  7.5 0.1 convolution_minimum_fusion.5
  7.6 0.2 convolution_minimum_fusion.4
  7.8 0.2 convolution_minimum_fusion.3
  7.9 0.2 convolution_minimum_fusion.2
  8.1 0.2 convolution_minimum_fusion.1
  8.3 0.3 compare_select_fusion
  8.5 0.1 broadcast_multiply_fusion
  8.6 0.8 sine_multiply_fusion
  9.4 0.7 tile.4
  10.1 0.1 broadcast_in_dim.152
  10.2 0.7 select_n.90.live_ref
  10.9 0.7 fusion.2.unpick_ref
  11.6 0.8 fusion.1.pick_ref
  12.5 86.7 %shard_map.91 = bf16[48,2048]{1,0:T(8,128)(2,1)} custom-call(bf16[48,2048]{1,0:T(8,128)(2,1)} %hidden_ref.1, bf16[384,192]{1,0:T(8,128)(2,1)} %fusion.1.pick_ref, bf16[192,384]{1,0:T(8,128)(2,1)} %fusion.2.unpick_ref, f32[48,128]{1,0:T(8,128)} %get-tuple-element.12.cosine_ref, f32[48,128]{1,0:T(8,128)} %get-tuple-element.11.sine_ref, f32[192,48]{1,0:T(8,128)} %bitcast.21, ...), custom_call_target="tpu_custom_call" | custom-call | tf_op jit(solution)/shard_map/pallas_call | solution.py:508
  99.2 1.6 %copy.15 = bf16[48,2048]{1,0:T(8,128)(2,1)} copy(bf16[48,2048]{1,0:T(8,128)(2,1)} %shard_map.91) | data formatting | bytes 393216
  (7 shorter events, 0.1 us)

commit v3 on v2

--- a/solution.py
+++ b/solution.py
@@ -3,6 +3,7 @@
 
 import jax
 import jax.numpy as jnp
+import numpy as np
 from jax import lax
 from jax.experimental import pallas as pl
 from jax.experimental.pallas import tpu as pltpu
@@ -20,29 +21,13 @@
 NEGATIVE = -1e30
 
 
-def lookup(table_vals, index_vals):
-    table_ids = jnp.arange(table_vals.shape[0], dtype=jnp.int32)
-    return jnp.sum(
-        jnp.where(index_vals[:, None] == table_ids[None, :], table_vals[None, :], 0), axis=1
-    )
-
-
-def ancestors(parents):
-    node_ids = jnp.arange(MOST_TREE_NODES, dtype=jnp.int32)
-    linked = (parents[..., :, None] == node_ids).astype(jnp.float32)
-    identity = (node_ids[:, None] == node_ids[None, :]).astype(jnp.float32)
-    closure = jnp.maximum(linked, identity)
-    for sweep in range((MOST_TREE_NODES - 1).bit_length()):
-        closure = jnp.minimum(jnp.matmul(closure, closure, precision=lax.Precision.HIGHEST), 1.0)
-    return closure
-
-
-def rotary(tree_depth):
-    half_ids = jnp.arange(HEAD_SIZE // 2, dtype=jnp.float32)
-    inv_freq = 1.0 / ROPE_BASE ** (half_ids * 2.0 / HEAD_SIZE)
-    angles = (tree_depth + CACHE_POSITIONS)[..., None] * inv_freq
-    angles = jnp.concatenate([angles, angles], axis=-1)
-    return (jnp.cos(angles), jnp.sin(angles))
+def rotary_tables():
+    half_ids = np.arange(HEAD_SIZE // 2, dtype=np.float32)
+    inv_freq = (1.0 / ROPE_BASE ** (half_ids * 2.0 / HEAD_SIZE)).astype(np.float32)
+    positions = np.arange(MOST_TREE_NODES, dtype=np.float32) + CACHE_POSITIONS
+    angles = (positions[:, None] * inv_freq).astype(np.float32).astype(np.float64)
+    cosine, sine = np.cos(angles), np.sin(angles)
+    return np.concatenate([cosine, cosine, -sine, sine], axis=1).astype(np.float32)
 
 
 MESH = pl.DeviceIdType.MESH
@@ -212,12 +197,11 @@
     core_inner,
     chunks,
     hidden_ref,
-    pick_ref,
-    unpick_ref,
-    cosine_ref,
-    sine_ref,
-    tree_ref,
-    live_ref,
+    rotary_ref,
+    block_live_ref,
+    parent_ref,
+    size_ref,
+    owner_ref,
     wq_ref,
     wkv_ref,
     cache_ref,
@@ -231,6 +215,9 @@
     kv_all,
     slots,
     mixed_rows,
+    pick_ref,
+    unpick_ref,
+    live_ref,
     load_sem,
     row_send,
     row_recv,
@@ -276,6 +263,25 @@
         "tensor", core_inner, lambda index: rows.at[row_span(index)], (row_send, row_recv)
     )
     row_gather.start()
+    requests = size_ref.shape[0]
+    sizes = [size_ref[r] for r in range(requests)]
+    owners = [owner_ref[s] for s in range(requests)]
+    slot_sizes, slot_starts = [], []
+    for owner in owners:
+        size, start = jnp.int32(0), jnp.int32(0)
+        for r in range(requests):
+            size = size + jnp.where(owner == r, sizes[r], 0)
+            start = start + jnp.where(owner > r, sizes[r], 0)
+        slot_sizes.append(size)
+        slot_starts.append(start)
+    row_total = rows.shape[0]
+    block_shape = (MOST_TREE_NODES, row_total)
+    block_nodes = lax.broadcasted_iota(jnp.int32, block_shape, 0)
+    block_lag = lax.broadcasted_iota(jnp.int32, block_shape, 1) - block_nodes
+    for s in range(requests):
+        pick_ref[s * MOST_TREE_NODES : (s + 1) * MOST_TREE_NODES, :] = jnp.where(
+            (block_lag == slot_starts[s]) & (block_nodes < slot_sizes[s]), 1.0, 0.0
+        ).astype(jnp.bfloat16)
     row_gather.forward()
     row_gather.finish()
 
@@ -331,14 +337,65 @@
         scatter.start(produce)
         scatters.append(scatter)
 
+    unpick_shape = unpick_ref.shape
+    slot_columns = lax.broadcasted_iota(jnp.int32, (1, unpick_shape[1]), 1)
+    lag = jnp.full((1, unpick_shape[1]), -unpick_shape[0] - unpick_shape[1], jnp.int32)
+    for s in range(requests):
+        nodes = slot_columns - s * MOST_TREE_NODES
+        inside = (nodes >= 0) & (nodes < slot_sizes[s])
+        lag = jnp.where(inside, slot_starts[s] - s * MOST_TREE_NODES, lag)
+    unpick_lag = lax.broadcasted_iota(
+        jnp.int32, unpick_shape, 0
+    ) - lax.broadcasted_iota(jnp.int32, unpick_shape, 1)
+    unpick_ref[...] = jnp.where(unpick_lag == lag, 1.0, 0.0).astype(jnp.bfloat16)
+
     scatters[0].forward()
+    tile = 1024
+    block_live = jnp.where(block_live_ref[...] > 0, 1.0, 0.0).astype(jnp.bfloat16)
+    block_live = jnp.broadcast_to(block_live, (16, block_live.shape[1]))
+
+    @pl.loop(0, cache.shape[0] // tile)
+    def _(i):
+        shape = (block_live.shape[1], tile)
+        offset = (
+            lax.broadcasted_iota(jnp.int32, shape, 1)
+            + i * tile
+            - lax.broadcasted_iota(jnp.int32, shape, 0) * CBLK
+        )
+        spread = jnp.where((offset >= 0) & (offset < CBLK), 1.0, 0.0).astype(jnp.bfloat16)
+        alive = jnp.dot(block_live, spread, preferred_element_type=jnp.float32)
+        live_ref[:, pl.ds(pl.multiple_of(i * tile, tile), tile)] = jnp.where(
+            alive[:1] > 0.5, 0.0, NEGATIVE
+        )
+
+    square = (MOST_TREE_NODES, MOST_TREE_NODES)
+    node_rows = lax.broadcasted_iota(jnp.int32, square, 0)
+    node_columns = lax.broadcasted_iota(jnp.int32, square, 1)
+    parents = parent_ref[pl.ds(owner_ref[slot], 1), :].astype(jnp.float32)
+    parents = jnp.sum(
+        jnp.where(node_rows == node_columns, parents, 0.0), axis=1, keepdims=True
+    ).astype(jnp.int32)
+    closure = jnp.where((node_rows == node_columns) | (node_columns == parents), 1.0, 0.0)
+    for sweep in range((MOST_TREE_NODES - 1).bit_length()):
+        link = closure.astype(jnp.bfloat16)
+        closure = jnp.minimum(jnp.dot(link, link, preferred_element_type=jnp.float32), 1.0)
+    depth = jnp.sum(closure, axis=1, keepdims=True).astype(jnp.int32) - 1
+    at_depth = jnp.where(node_columns == depth, 1.0, 0.0)
+    rotary = jnp.dot(
+        at_depth,
+        rotary_ref[...],
+        preferred_element_type=jnp.float32,
+        precision=lax.Precision.HIGHEST,
+    )
+    cosine, sine = rotary[:, :HEAD_SIZE], rotary[:, HEAD_SIZE:]
+    tree_bias = jnp.where(closure > 0.5, 0.0, NEGATIVE)
+    tree_bias = jnp.concatenate([tree_bias] * chunk_heads, axis=0)
     scatters[1].forward()
     kv_all[me] = scatters[0].finish()
     kv_gather = Gather(
         "tensor", tensor_count, lambda index: kv_all.at[index], (kv_send, kv_recv)
     )
     kv_gather.start()
-    cosine, sine = cosine_ref[...], sine_ref[...]
 
     def rotated(values):
         widened = values.astype(jnp.float32)
@@ -373,7 +430,6 @@
             * score_scale
         )
 
-    tile = 1024
     gathers = []
     for c in range(chunks):
         if c + 1 < chunks:
@@ -383,7 +439,7 @@
             [rotated(found[:, h * HEAD_SIZE : (h + 1) * HEAD_SIZE]) for h in range(chunk_heads)],
             axis=0,
         )
-        scores = scored(query, tree_key) + tree_ref[...]
+        scores = scored(query, tree_key) + tree_bias
         top = jnp.max(scores, axis=1, keepdims=True)
         weights = jnp.exp(scores - top)
         total = jnp.sum(weights, axis=1, keepdims=True)
@@ -508,7 +564,7 @@
     return pl.pallas_call(
         functools.partial(kernel, req_inner, core_inner, chunks),
         out_shape=jax.ShapeDtypeStruct((rows_here, out_columns), bf16),
-        in_specs=[vmem] * 7 + [any_space] * 4,
+        in_specs=[vmem] * 4 + [pl.BlockSpec(memory_space=pltpu.SMEM)] * 2 + [any_space] * 4,
         out_specs=vmem,
         scratch_shapes=[
             pltpu.VMEM((row_total, width), bf16),
@@ -519,6 +575,9 @@
             pltpu.VMEM((tensor_count, MOST_TREE_NODES, kv_columns), bf16),
             pltpu.VMEM((req_count * MOST_TREE_NODES, depth), bf16),
             pltpu.VMEM((row_total, depth), bf16),
+            pltpu.VMEM((req_count * MOST_TREE_NODES, row_total), bf16),
+            pltpu.VMEM((row_total, req_count * MOST_TREE_NODES), bf16),
+            pltpu.VMEM((1, CACHE_POSITIONS), jnp.float32),
             dma((4,)),
         ]
         + [dma((count,)) for count in sems for both in range(2)]
@@ -540,49 +599,7 @@
     tree_parent,
     slot_request,
 ):
-    tensor_count = lax.axis_size("tensor")
-    req_index = lax.axis_index("req")
-    resident_requests = keyvalue_cache.shape[0]
-    resident_slots = resident_requests * MOST_TREE_NODES
-    row_total = hidden.shape[0] * tensor_count
-    row_ends = jnp.cumsum(tree_size)
-    starts = row_ends - tree_size
-    request_ids = jnp.arange(tree_size.shape[0], dtype=jnp.int32)
-    home_slot = jnp.sum(
-        jnp.where(slot_request[None, :] == request_ids[:, None], request_ids[None, :], 0), axis=1
-    )
-    slot_ids = jnp.arange(resident_slots * lax.axis_size("req"), dtype=jnp.int32)
-    owner_req = lookup(slot_request, slot_ids // MOST_TREE_NODES)
-    node_ids = slot_ids % MOST_TREE_NODES
-    is_valid = node_ids < lookup(tree_size, owner_req)
-    row_ids = jnp.minimum(lookup(starts, owner_req) + node_ids, row_total - 1)
-    all_rows = jnp.arange(row_total, dtype=jnp.int32)
-    pick_rows = (
-        (row_ids[:, None] == all_rows[None, :]) & is_valid[:, None]
-    ).astype(jnp.bfloat16)
-    my_requests = lax.dynamic_slice_in_dim(
-        slot_request, req_index * resident_requests, resident_requests
-    )
-    parents = jnp.sum(
-        jnp.where(
-            my_requests[:, None, None] == request_ids[None, :, None], tree_parent[None, :, :], 0
-        ),
-        axis=1,
-    )
-    closure = ancestors(parents)
-    tree_depth = jnp.sum(closure, axis=-1) - 1.0
-    cosine_table, sine_table = rotary(tree_depth.reshape(resident_slots))
-    signed_sine = sine_table * jnp.where(jnp.arange(HEAD_SIZE) < HEAD_SIZE // 2, -1.0, 1.0)
-    tree_bias = jnp.tile(jnp.where(closure[0] > 0.5, 0.0, NEGATIVE), (CHUNK_HEADS, 1))
-    live_bias = jnp.where(jnp.repeat(cache_live, CBLK, axis=1) > 0, 0.0, NEGATIVE)
-    row_ids = all_rows
-    owner_req = jnp.sum((row_ends[None, :] <= row_ids[:, None]).astype(jnp.int32), axis=1)
-    slot_ids = lookup(home_slot, owner_req) * MOST_TREE_NODES + row_ids - lookup(starts, owner_req)
-    all_slots = jnp.arange(
-        resident_slots * lax.axis_size("req"), dtype=jnp.int32
-    )
-    pick_slots = (slot_ids[:, None] == all_slots[None, :]).astype(jnp.bfloat16)
-    tables = (pick_rows, pick_slots, cosine_table, signed_sine, tree_bias, live_bias)
+    tables = (rotary_tables(), cache_live, tree_parent, tree_size, slot_request)
     return run(hidden, tables, w_query, keyvalue_weight, keyvalue_cache[0], w_out)
 
 

time: 101 us -> 88.4 us (0.88)
  other arithmetic: 8.66 us -> 0 us
  local copies, waits for them, and re-layouts: 4.31 us -> 1.62 us
  matrix products: 1.02 us -> 0 us
    reduce_sum x6 -> x0, other arithmetic: 3.2 us -> none  [the longest x3 1.57 us: lookup(): jnp.sum(jnp.where(index_vals[:, None] == table_ids[None, :], table_vals[N...]
    convert_element_type x2 -> x0, other arithmetic: 1.59 us -> none  [the longest x1 0.85 us: body(): pick_rows = ((row_ids[:, None] == all_rows[None, :]) & is_valid[:, None])...]
    dynamic_slice x1 -> x0, local copies, waits for them, and re-layouts: 1.24 us -> none  [body(): lax.dynamic_slice_in_dim(slot_request, req_index * resident_requests, res...]
    dot_general x6 -> x0, matrix products: 1.02 us -> none  [ancestors(): jnp.matmul(closure, closure, precision=lax.Precision.HIGHEST)]
where the time goes in v3:
time: 88.4 us; the launch traced here: 88.2 us
  Pallas kernels  86.6 us (98%)
  local copies, waits for them, and re-layouts  1.62 us (2%)
    pallas_call x1, Pallas kernels, run(): pl.pallas_call(functools.partial(kernel, req_inner, core_inner, chunks),...  86.6 us

profile of v3, /device:TPU:0, one launch (start us, length us, event | category | flops | bytes accessed | tf_op | source)
XLA Modules:
  0.0 88.2 jit_solution(7879972964180083807)
XLA Ops:
  0.0 86.6 %shard_map.100 = bf16[48,2048]{1,0:T(8,128)(2,1)} custom-call(bf16[48,2048]{1,0:T(8,128)(2,1)} %hidden_ref.1, f32[48,256]{1,0:T(8,128)} %constant.2.clone.rotary_ref, s32[1,256]{1,0:T(1,128)} %block_live_ref.1, s32[8,48]{1,0:T(8,128)} %parent_ref.1, s32[8]{0:T(128)} %size_ref.1, s32[8]{0:T(128)} %owner_ref.1, bf16[2048,2048]{1,0:T(8,128)(2,1)} %wq_ref.1, ...), custom_call_target="tpu_custom_call" | custom-call | tf_op jit(solution)/shard_map/pallas_call | solution.py:564
  86.6 1.6 %copy.12 = bf16[48,2048]{1,0:T(8,128)(2,1)} copy(bf16[48,2048]{1,0:T(8,128)(2,1)} %shard_map.100) | data formatting | bytes 393216

commit v4 on v3

--- a/solution.py
+++ b/solution.py
@@ -263,6 +263,24 @@
         "tensor", core_inner, lambda index: rows.at[row_span(index)], (row_send, row_recv)
     )
     row_gather.start()
+
+    def cache_part(owner, reader):
+        head = reader * heads_here // group_size
+        return (
+            cache_ref.at[:, pl.ds(pl.multiple_of(head * pair, pair), pair)],
+            cache.at[pl.ds(pl.multiple_of(owner * positions, positions), positions)],
+        )
+
+    own_cache = pltpu.make_async_copy(*cache_part(me, me), load_sem.at[3])
+    own_cache.start()
+    cache_sems = (cache_send, cache_recv)
+    cache_copies = []
+    for step in range(1, tensor_count):
+        reader = lax.rem(me + step, tensor_count)
+        copy = remote(*cache_part(me, reader), cache_sems, step, "tensor", reader)
+        copy.start()
+        cache_copies.append(copy)
+
     requests = size_ref.shape[0]
     sizes = [size_ref[r] for r in range(requests)]
     owners = [owner_ref[s] for s in range(requests)]
@@ -284,23 +302,6 @@
         ).astype(jnp.bfloat16)
     row_gather.forward()
     row_gather.finish()
-
-    def cache_part(owner, reader):
-        head = reader * heads_here // group_size
-        return (
-            cache_ref.at[:, pl.ds(pl.multiple_of(head * pair, pair), pair)],
-            cache.at[pl.ds(pl.multiple_of(owner * positions, positions), positions)],
-        )
-
-    own_cache = pltpu.make_async_copy(*cache_part(me, me), load_sem.at[3])
-    own_cache.start()
-    cache_sems = (cache_send, cache_recv)
-    cache_copies = []
-    for step in range(1, tensor_count):
-        reader = lax.rem(me + step, tensor_count)
-        copy = remote(*cache_part(me, reader), cache_sems, step, "tensor", reader)
-        copy.start()
-        cache_copies.append(copy)
 
     scatters = []
     for c in range(chunks + 1):
@@ -404,6 +405,8 @@
         )
         return (widened * cosine + turned * sine).astype(jnp.bfloat16)
 
+    for c in range(2, min(chunks, 3) + 1):
+        scatters[c].forward()
     kv_gather.finish()
     kv_head = me * heads_here // group_size
     kv_columns = kv_all.shape[2]
@@ -432,8 +435,8 @@
 
     gathers = []
     for c in range(chunks):
-        if c + 1 < chunks:
-            scatters[c + 2].forward()
+        if c + 3 < chunks:
+            scatters[c + 4].forward()
         found = scatters[c + 1].finish()
         query = jnp.concatenate(
             [rotated(found[:, h * HEAD_SIZE : (h + 1) * HEAD_SIZE]) for h in range(chunk_heads)],

time: 88.4 us -> 77.1 us (0.87)
  Pallas kernels: 86.6 us -> 75.3 us
    pallas_call x1, Pallas kernels: 86.6 us -> 75.3 us  [run(): pl.pallas_call(functools.partial(kernel, req_inner, core_inner, chunks),...]
where the time goes in v4:
time: 77.1 us; the launch traced here: 76.9 us
  Pallas kernels  75.3 us (98%)
  local copies, waits for them, and re-layouts  1.62 us (2%)
    pallas_call x1, Pallas kernels, run(): pl.pallas_call(functools.partial(kernel, req_inner, core_inner, chunks),...  75.3 us
    unnamed x1, local copies, waits for them, and re-layouts  1.62 us

profile of v4, /device:TPU:0, one launch (start us, length us, event | category | flops | bytes accessed | tf_op | source)
XLA Modules:
  0.0 76.9 jit_solution(574493966777702432)
XLA Ops:
  0.0 75.3 %shard_map.100 = bf16[48,2048]{1,0:T(8,128)(2,1)} custom-call(bf16[48,2048]{1,0:T(8,128)(2,1)} %hidden_ref.1, f32[48,256]{1,0:T(8,128)} %constant.2.clone.rotary_ref, s32[1,256]{1,0:T(1,128)} %block_live_ref.1, s32[8,48]{1,0:T(8,128)} %parent_ref.1, s32[8]{0:T(128)} %size_ref.1, s32[8]{0:T(128)} %owner_ref.1, bf16[2048,2048]{1,0:T(8,128)(2,1)} %wq_ref.1, ...), custom_call_target="tpu_custom_call" | custom-call | tf_op jit(solution)/shard_map/pallas_call | solution.py:567
  75.3 1.6 %copy.12 = bf16[48,2048]{1,0:T(8,128)(2,1)} copy(bf16[48,2048]{1,0:T(8,128)(2,1)} %shard_map.100) | data formatting | bytes 393216

commit v5 on v4

--- a/solution.py
+++ b/solution.py
@@ -435,8 +435,6 @@
 
     gathers = []
     for c in range(chunks):
-        if c + 3 < chunks:
-            scatters[c + 4].forward()
         found = scatters[c + 1].finish()
         query = jnp.concatenate(
             [rotated(found[:, h * HEAD_SIZE : (h + 1) * HEAD_SIZE]) for h in range(chunk_heads)],
@@ -484,6 +482,8 @@
             c * req_count,
         )
         gather.start()
+        if c + 3 < chunks:
+            scatters[c + 4].forward()
         if gathers:
             gathers[-1].forward()
         gathers.append(gather)

time: 77.1 us -> 81 us (1.051)
  Pallas kernels: 75.3 us -> 79.2 us
    pallas_call x1, Pallas kernels: 75.3 us -> 79.2 us  [run(): pl.pallas_call(functools.partial(kernel, req_inner, core_inner, chunks),...]
where the time goes in v5:
time: 81 us; the launch traced here: 80.9 us
  Pallas kernels  79.2 us (98%)
  local copies, waits for them, and re-layouts  1.62 us (2%)
    pallas_call x1, Pallas kernels, run(): pl.pallas_call(functools.partial(kernel, req_inner, core_inner, chunks),...  79.2 us

profile of v5, /device:TPU:0, one launch (start us, length us, event | category | flops | bytes accessed | tf_op | source)
XLA Modules:
  0.0 80.9 jit_solution(18008849790768071012)
XLA Ops:
  0.0 79.2 %shard_map.100 = bf16[48,2048]{1,0:T(8,128)(2,1)} custom-call(bf16[48,2048]{1,0:T(8,128)(2,1)} %hidden_ref.1, f32[48,256]{1,0:T(8,128)} %constant.2.clone.rotary_ref, s32[1,256]{1,0:T(1,128)} %block_live_ref.1, s32[8,48]{1,0:T(8,128)} %parent_ref.1, s32[8]{0:T(128)} %size_ref.1, s32[8]{0:T(128)} %owner_ref.1, bf16[2048,2048]{1,0:T(8,128)(2,1)} %wq_ref.1, ...), custom_call_target="tpu_custom_call" | custom-call | tf_op jit(solution)/shard_map/pallas_call | solution.py:567
  79.3 1.6 %copy.12 = bf16[48,2048]{1,0:T(8,128)(2,1)} copy(bf16[48,2048]{1,0:T(8,128)(2,1)} %shard_map.100) | data formatting | bytes 393216
